TPU v7x, 768 devices: a whole 4x8x12 slice. The times are simulated.
768 devices in a mesh: row: 32 (over z_hi, x, core), col: 24 (over z_lo, y).
Axes of the slice: x: 4, y: 8, z: 12 (z_hi: 4, z_lo: 3; z = z_hi * 3 + z_lo), core: 2. Of those that a mesh axis runs over, the one named last changes fastest.
Arguments:
- img_raw: bfloat16 [18432, 1152], P(('row', 'col')), may hold values from -0.1875 to 0.1875
- txt_raw: bfloat16 [18432, 1152], P(('col', 'row')), may hold values from -0.1875 to 0.1875
- labels: int32 [18432], P(('row', 'col')), may hold values from 0 to 18431, each once
- log_logit_scale: float32 [1], replicated, may hold values from 1 to 1.6
- bias: float32 [1], replicated, may hold values from -3 to -1.5
Outputs:
- img_grad: float32 [18432, 1152], P(('row', 'col'))
- txt_grad: float32 [18432, 1152], P(('col', 'row'))
Inputs may be any that keep to these rules, and one draw needn't show every extreme that they name: labels is a permutation: every text is the positive of exactly one image.
All inputs are finite; a program needn't handle non-finite values.
Results may differ from a plain program's by a relative error of at most 0.0043.
Values may be sent and summed in bfloat16 or wider, within the bound.
No kernel may reach another device: no remote copies, remote signals or barrier semaphores. Data moves between devices by JAX's collectives and lax.ppermute only.
A program may use at most 32 MiB of HBM per device.

v0:
```python
import jax
import jax.numpy as jnp
from jax import lax
from jax.sharding import PartitionSpec as P

EPS = 1e-06


def normalize(raw):
    wide = raw.astype(jnp.float32)
    inverse = lax.rsqrt(jnp.sum(wide * wide, axis=-1, keepdims=True) + EPS)
    return (wide * inverse, inverse)


def project_back(hat, inverse, dnorm):
    return (dnorm - hat * jnp.sum(hat * dnorm, axis=-1, keepdims=True)) * inverse


def block_gradients(
    picture_portion, target_portion, caption_portion, column_begin, logit_scaling, block_shift
):
    pair_logits = lax.dot_general(
        picture_portion,
        caption_portion,
        (((1,), (1,)), ((), ())),
        preferred_element_type=jnp.float32,
    )
    columns = column_begin + jnp.arange(caption_portion.shape[0], dtype=jnp.int32)
    matching_pair_mask = (target_portion[:, None] == columns[None, :]).astype(jnp.float32)
    return (jax.nn.sigmoid(logit_scaling * pair_logits + block_shift) - matching_pair_mask).astype(
        jnp.bfloat16
    )


def on_device(img_raw, txt_raw, labels, log_logit_scale, bias):
    logit_scaling = jnp.exp(log_logit_scale[0])
    block_shift = bias[0]
    img_hat, img_inv = normalize(img_raw)
    txt_hat, txt_inv = normalize(txt_raw)
    picture_rows, target_rows = (
        lax.all_gather(img_hat.astype(jnp.bfloat16), "col", axis=0, tiled=True),
        lax.all_gather(labels, "col", axis=0, tiled=True),
    )
    caption_columns = lax.all_gather(txt_hat.astype(jnp.bfloat16), "row", axis=0, tiled=True)
    block_begin = lax.axis_index("col") * caption_columns.shape[0]
    gradient_block = block_gradients(
        picture_rows, target_rows, caption_columns, block_begin, logit_scaling, block_shift
    )
    part = gradient_block
    img_dnorm = lax.psum_scatter(
        logit_scaling * jnp.dot(part, caption_columns, preferred_element_type=jnp.float32),
        "col",
        scatter_dimension=0,
        tiled=True,
    )
    part = gradient_block
    txt_dnorm = lax.psum_scatter(
        logit_scaling
        * lax.dot_general(
            part, picture_rows, (((0,), (0,)), ((), ())), preferred_element_type=jnp.float32
        ),
        "row",
        scatter_dimension=0,
        tiled=True,
    )
    img_grad = project_back(img_hat, img_inv, img_dnorm)
    txt_grad = project_back(txt_hat, txt_inv, txt_dnorm)
    return (img_grad, txt_grad)


def solution(mesh):
    return jax.shard_map(
        on_device,
        mesh=mesh,
        in_specs=(P(("row", "col"), None), P(("col", "row"), None), P(("row", "col")), P(), P()),
        out_specs=(P(("row", "col"), None), P(("col", "row"), None)),
        check_vma=False,
    )
```

profile of v0, /device:TPU:6, one launch (start us, length us, event | category | flops | bytes accessed | tf_op | source)
XLA Modules:
  0.0 485.3 jit_solution(8272274457299603268)
XLA Ops:
  7.2 0.0 all-gather.3.cloned.1.call-start
  7.2 0.9 fusion.9
  8.2 1.5 fusion.5
  9.7 0.0 all-gather.3.cloned.1.call-update
  9.7 0.0 all-gather.5.cloned.1.call-start
  9.7 0.9 fusion.13
  10.7 1.5 fusion.2
  12.2 0.0 reduce-scatter.8.cloned.1.call-start
  13.6 1.4 dynamic-slice
  15.7 0.9 dynamic-update-slice
  16.6 57.8 %all-reduce = s32[576]{0:T(1024)S(1)} all-reduce(s32[576]{0:T(1024)S(1)} %dynamic-update-slice), channel_id=1, replica_groups=mesh['row'=32,'col'=24] {'col'}, use_global_device_ids=true, to_apply=%add | all-reduce | flops 576 | bytes 4608
  74.3 57.4 %all-gather.3.cloned.1.call-done = bf16[576,1152]{1,0:T(8,128)(2,1)} async-done(((bf16[24,1152]{1,0:T(8,128)(2,1)}), bf16[576,1152]{1,0:T(8,128)(2,1)}) %all-gather.3.cloned.1.call-update) | async-done | bytes 1327120 | tf_op jit(solution)/shard_map/all_gather | solution.py:41
  131.7 82.3 %all-gather.5.cloned.1.call-done = bf16[768,1152]{1,0:T(8,128)(2,1)} async-done(((bf16[24,1152]{1,0:T(8,128)(2,1)}), bf16[768,1152]{1,0:T(8,128)(2,1)}) %all-gather.5.cloned.1.call-update) | async-done | bytes 1769488 | tf_op jit(solution)/shard_map/all_gather | solution.py:44
  214.0 3.5 subtract_convert_fusion
  217.6 2.8 convolution_multiply_fusion.1
  220.4 0.0 reduce-scatter.10.cloned.1.call-start
  220.5 1.2 copy-done.3
  221.7 3.5 convolution_multiply_fusion
  225.2 113.4 %reduce-scatter.8.cloned.1.call-done = f32[24,1152]{1,0:T(8,128)} async-done(((f32[576,1152]{1,0:T(8,128)}), f32[24,1152]{1,0:T(8,128)}) %reduce-scatter.8.cloned.1.call-update) | async-done | bytes 110608
  338.6 1.1 fusion.6
  339.7 1.6 fusion.8
  341.3 134.7 %reduce-scatter.10.cloned.1.call-done = f32[24,1152]{1,0:T(8,128)} async-done(((f32[768,1152]{1,0:T(8,128)}), f32[24,1152]{1,0:T(8,128)}) %reduce-scatter.10.cloned.1.call-update) | async-done | bytes 110608
  476.0 1.1 fusion.10
  477.1 1.6 fusion.12
  (14 shorter events, 0.1 us)
Async XLA Ops:
  7.2 124.6 %all-gather.3.cloned.1.call-start = ((), (), s32[]{:S(2)}) async-start(), calls=%async_computation.2 | async-start | bytes 1382400 | tf_op jit(solution)/shard_map/all_gather | solution.py:41
  9.7 204.3 %all-gather.5.cloned.1.call-start = ((), (), s32[]{:S(2)}) async-start(), calls=%async_computation.3 | async-start | bytes 1824768 | tf_op jit(solution)/shard_map/all_gather | solution.py:44
  12.2 326.3 %reduce-scatter.8.cloned.1.call-start = ((), (), s32[]{:S(2)}) async-start(), calls=%async_computation.4 | async-start | bytes 2764800
  214.0 3.5 copy-start.2
  220.4 1.3 copy-start.3
  220.4 255.6 %reduce-scatter.10.cloned.1.call-start = ((), (), s32[]{:S(2)}) async-start(), calls=%async_computation.5 | async-start | bytes 3649536
  225.2 113.4 %copy-start = (bf16[24,1152]{1,0:T(8,128)(2,1)S(1)}, bf16[24,1152]{1,0:T(8,128)(2,1)}, u32[]{:S(2)}) copy-start(bf16[24,1152]{1,0:T(8,128)(2,1)} %param.5) | copy-start | bytes 165892
  225.2 250.9 %copy-start.1 = (bf16[24,1152]{1,0:T(8,128)(2,1)S(1)}, bf16[24,1152]{1,0:T(8,128)(2,1)}, u32[]{:S(2)}) copy-start(bf16[24,1152]{1,0:T(8,128)(2,1)} %param.6) | copy-start | bytes 165892
Sparse Core Ops, SparseCore 0:
  11.0 120.7 all-gather.2
  136.0 77.9 all-gather.4
  220.5 117.9 reduce-scatter.7
  344.5 131.5 reduce-scatter.9
where the time goes:
time: 486 us; the launch traced here: 485 us
  waiting for transfers between devices  388 us (80%)
  blocking collectives  57.8 us (12%)
  between operations  15.8 us (3%)
  other arithmetic  10.4 us (2%)
  matrix products  9.8 us (2%)
    unnamed x6, waiting for transfers between devices  248 us
    all_gather x1, waiting for transfers between devices, on_device(): lax.all_gather(txt_hat.astype(jnp.bfloat16), 'row', axis=0, tiled=True)  82.3 us
    unnamed x1, blocking collectives  57.8 us
    all_gather x1, waiting for transfers between devices, on_device(): lax.all_gather(img_hat.astype(jnp.bfloat16), 'col', axis=0, tiled=True)  57.4 us
  transfers between devices with their start and end apart: 4, of which 4 were waited for; matrix products, arithmetic and copies ran while one was open for 2% of the time, Pallas kernels for 0%

commit v1 on v0

v1 whole, which is shorter than its diff:
```python
import jax
import jax.numpy as jnp
from jax import lax
from jax.sharding import Mesh, PartitionSpec as P

EPS = 1e-06
BF = jnp.bfloat16
F32 = jnp.float32
SWAP = [(0, 1), (1, 0)]


def normalize(raw):
    wide = raw.astype(F32)
    inverse = lax.rsqrt(jnp.sum(wide * wide, axis=-1, keepdims=True) + EPS)
    return (wide * inverse, inverse)


def project_back(hat, inverse, dnorm):
    return (dnorm - hat * jnp.sum(hat * dnorm, axis=-1, keepdims=True)) * inverse


def exchange(blocks, axes):
    return lax.all_to_all(blocks, axes, split_axis=0, concat_axis=0, tiled=True)


def spread(block, axes, count):
    return exchange(jnp.broadcast_to(block[None], (count,) + block.shape), axes)


def on_device(img_raw, txt_raw, labels, log_logit_scale, bias):
    blk, width = img_raw.shape
    n_zh, n_x, n_zl, n_y = (lax.axis_size(a) for a in ("zh", "x", "zl", "y"))
    temperature = jnp.exp(log_logit_scale[0])
    shift = bias[0]
    img_hat, img_inv = normalize(img_raw)
    txt_hat, txt_inv = normalize(txt_raw)

    high = labels // 256
    tail = jnp.stack([high, labels - 256 * high], axis=1).astype(BF)
    tail = jnp.pad(tail, ((0, 0), (0, 126)))
    packed = jnp.concatenate([img_hat.astype(BF), tail], axis=1)
    packed = spread(packed, "zl", n_zl)
    packed, txt_block = lax.optimization_barrier((packed, txt_hat.astype(BF)))
    packed = lax.all_gather(packed.reshape(n_zl * blk, -1), "y", axis=0, tiled=True)
    txt_own = spread(txt_block, ("zh", "x"), n_zh * n_x).reshape(n_zh * n_x * blk, width)
    txt_far = lax.ppermute(txt_own, "c", SWAP)

    img = packed[:, :width]
    marks = packed[:, width : width + 2].astype(F32)
    target = (marks[:, :1] * 256.0 + marks[:, 1:]).astype(jnp.int32)

    column_block = (lax.axis_index("zl") * n_y + lax.axis_index("y")) * (n_zh * n_x * 2)
    core = lax.axis_index("c")
    place = jnp.arange(n_zh * n_x * blk, dtype=jnp.int32)

    def pair_grad(txt, half):
        scores = lax.dot_general(img, txt, (((1,), (1,)), ((), ())), preferred_element_type=F32)
        columns = (column_block + (place // blk) * 2 + half) * blk + place % blk
        positive = (target == columns[None, :]).astype(F32)
        return (jax.nn.sigmoid(temperature * scores + shift) - positive).astype(BF)

    grad_own = pair_grad(txt_own, core)
    grad_far = pair_grad(txt_far, 1 - core)

    def txt_part(grad):
        return temperature * lax.dot_general(
            grad, img, (((0,), (0,)), ((), ())), preferred_element_type=F32
        )

    arrived = lax.ppermute(txt_part(grad_far).astype(BF), "c", SWAP)
    txt_sum = txt_part(grad_own) + arrived.astype(F32)
    txt_blocks = exchange(txt_sum.astype(BF).reshape(n_zh * n_x, blk, width), ("zh", "x"))
    txt_dnorm = jnp.sum(txt_blocks.astype(F32), axis=0)

    img_sum = temperature * (
        jnp.dot(grad_own, txt_own, preferred_element_type=F32)
        + jnp.dot(grad_far, txt_far, preferred_element_type=F32)
    )
    img_blocks = exchange(img_sum.astype(BF).reshape(n_y * n_zl, blk, width), ("y", "zl"))
    img_dnorm = jnp.sum(img_blocks.astype(F32), axis=0)

    return (project_back(img_hat, img_inv, img_dnorm), project_back(txt_hat, txt_inv, txt_dnorm))


def solution(mesh):
    fine = Mesh(mesh.devices.reshape(4, 4, 2, 3, 8), ("zh", "x", "c", "zl", "y"))
    row, col = ("zh", "x", "c"), ("zl", "y")
    return jax.shard_map(
        on_device,
        mesh=fine,
        in_specs=(P(row + col, None), P(col + row, None), P(row + col), P(), P()),
        out_specs=(P(row + col, None), P(col + row, None)),
        check_vma=False,
    )
```

time: 486 us -> 196 us (0.40)
  the two profiles are of different devices: /device:TPU:6 before, /device:TPU:256 now
where the time goes in v1:
time: 196 us
  waiting for transfers between devices  119 us (61%)
  starting transfers between devices  42.1 us (21%)
  between operations  15.5 us (8%)
  matrix products  9.14 us (5%)
  other arithmetic  8.42 us (4%)
    all_to_all x4, waiting for transfers between devices, exchange(): return lax.all_to_all(blocks, axes, split_axis=0, concat_axis=0, tiled=True)  102 us
    all_to_all x4, starting transfers between devices, exchange(): return lax.all_to_all(blocks, axes, split_axis=0, concat_axis=0, tiled=True)  38.2 us
    all_gather x1, waiting for transfers between devices, on_device(): lax.all_gather(packed.reshape(n_zl * blk, -1), 'y', axis=0, tiled=True)  14.4 us
  transfers between devices with their start and end apart: 7, of which 6 were waited for; matrix products, arithmetic and copies ran while one was open for 4% of the time, Pallas kernels for 0%

profile of v1, /device:TPU:256, one launch (start us, length us, event | category | flops | bytes accessed | tf_op | source)
XLA Modules:
  0.0 195.6 jit_solution(16997259694653031125)
XLA Ops:
  7.2 0.9 fusion.33
  8.1 0.9 fusion.28
  11.1 6.3 %all-to-all-start = ((bf16[3,24,1280]{2,1,0:T(8,128)(2,1)}), bf16[3,24,1280]{2,1,0:T(8,128)(2,1)S(1)}, u32[]{:S(2)}, u32[]{:S(2)}) async-start(bf16[3,24,1280]{2,1,0:T(8,128)(2,1)} %broadcast_in_dim.4), calls=%async_computation | async-start | bytes 368640 | tf_op jit(solution)/shard_map/all_to_all | solution.py:23
  17.5 0.9 fusion.37
  18.4 0.9 fusion.25
  19.3 2.7 %all-to-all-done = bf16[3,24,1280]{2,1,0:T(8,128)(2,1)S(1)} async-done(((bf16[3,24,1280]{2,1,0:T(8,128)(2,1)}), bf16[3,24,1280]{2,1,0:T(8,128)(2,1)S(1)}, u32[]{:S(2)}, u32[]{:S(2)}) %all-to-all-start) | async-done | bytes 184352 | tf_op jit(solution)/shard_map/all_to_all | solution.py:23
  22.0 1.0 broadcast_in_dim.5
  23.0 13.0 %all-to-all-start.1 = ((bf16[16,24,1152]{2,1,0:T(8,128)(2,1)}), bf16[16,24,1152]{2,1,0:T(8,128)(2,1)S(1)}, u32[]{:S(2)}, u32[]{:S(2)}) async-start(bf16[16,24,1152]{2,1,0:T(8,128)(2,1)} %broadcast_in_dim.5), calls=%async_computation.1 | async-start | bytes 1769472 | tf_op jit(solution)/shard_map/all_to_all | solution.py:23
  36.7 31.9 %all-to-all-done.1 = bf16[16,24,1152]{2,1,0:T(8,128)(2,1)S(1)} async-done(((bf16[16,24,1152]{2,1,0:T(8,128)(2,1)}), bf16[16,24,1152]{2,1,0:T(8,128)(2,1)S(1)}, u32[]{:S(2)}, u32[]{:S(2)}) %all-to-all-start.1) | async-done | bytes 884768 | tf_op jit(solution)/shard_map/all_to_all | solution.py:23
  68.7 1.9 collective-permute-start
  71.9 14.4 %all-gather.2.cloned.1.call-done = bf16[576,1280]{1,0:T(8,128)(2,1)} async-done(((bf16[72,1280]{1,0:T(8,128)(2,1)}), bf16[576,1280]{1,0:T(8,128)(2,1)}) %all-gather.2.cloned.1.call-update) | async-done | bytes 1474576 | tf_op jit(solution)/shard_map/all_gather | solution.py:44
  86.4 0.9 slice_convert_fusion
  87.6 2.4 %fusion.15 = bf16[576,384]{1,0:T(8,128)(2,1)S(1)} fusion(bf16[384,1152]{1,0:T(8,128)(2,1)S(1)} %collective-permute-done, bf16[576,1280]{1,0:T(8,128)(2,1)} %all-gather.2.cloned.1.call-done, s32[384]{0:T(512)S(1)} %multiply_add_fusion, f32[]{:T(128)} %bitcast.19, f32[]{:T(128)} %bitcast, s32[576]{0:T(1024)S(1)} %fusion.22), kind=kOutput, calls=%fused_computation.23 | convolution fusion | flops 511598592 | bytes 2659072 | tf_op jit(solution)/shard_map/dot_general | solution.py:57
  90.0 0.9 fusion.2
  91.0 1.9 collective-permute-start.1
  92.9 1.0 fusion.16
  93.9 1.4 collective-permute-done.1
  95.3 1.9 add_convert_fusion
  97.2 11.7 %all-to-all-start.3 = ((bf16[16,24,1152]{2,1,0:T(8,128)(2,1)}), bf16[16,24,1152]{2,1,0:T(8,128)(2,1)S(1)}, u32[]{:S(2)}, u32[]{:S(2)}) async-start(bf16[16,24,1152]{2,1,0:T(8,128)(2,1)} %bitcast.7), calls=%async_computation.3 | async-start | bytes 1769472 | tf_op jit(solution)/shard_map/all_to_all | solution.py:23
  108.9 0.9 fusion.48
  109.8 2.0 %fusion.1 = bf16[576,1152]{1,0:T(8,128)(2,1)} fusion(f32[576,1152]{1,0:T(8,128)S(1)} %fusion.48, bf16[576,384]{1,0:T(8,128)(2,1)S(1)} %fusion.15, bf16[384,1152]{1,0:T(8,128)(2,1)S(1)} %collective-permute-done, f32[]{:T(128)} %bitcast), kind=kOutput, calls=%fused_computation.4 | convolution fusion | flops 511598592 | bytes 5308420 | tf_op jit(solution)/shard_map/dot_general | solution.py:77
  111.8 31.3 %all-to-all-done.3 = bf16[16,24,1152]{2,1,0:T(8,128)(2,1)S(1)} async-done(((bf16[16,24,1152]{2,1,0:T(8,128)(2,1)}), bf16[16,24,1152]{2,1,0:T(8,128)(2,1)S(1)}, u32[]{:S(2)}, u32[]{:S(2)}) %all-to-all-start.3) | async-done | bytes 884768 | tf_op jit(solution)/shard_map/all_to_all | solution.py:23
  143.1 7.2 %all-to-all-start.2 = ((bf16[24,24,1152]{2,1,0:T(8,128)(2,1)}), bf16[24,24,1152]{2,1,0:T(8,128)(2,1)S(1)}, u32[]{:S(2)}, u32[]{:S(2)}) async-start(bf16[24,24,1152]{2,1,0:T(8,128)(2,1)} %bitcast.6), calls=%async_computation.2 | async-start | bytes 2654208 | tf_op jit(solution)/shard_map/all_to_all | solution.py:23
  151.4 36.2 %all-to-all-done.2 = bf16[24,24,1152]{2,1,0:T(8,128)(2,1)S(1)} async-done(((bf16[24,24,1152]{2,1,0:T(8,128)(2,1)}), bf16[24,24,1152]{2,1,0:T(8,128)(2,1)S(1)}, u32[]{:S(2)}, u32[]{:S(2)}) %all-to-all-start.2) | async-done | bytes 1327136 | tf_op jit(solution)/shard_map/all_to_all | solution.py:23
  (28 shorter events, 5.3 us)
Async XLA Ops:
  11.1 10.8 %all-to-all-start = ((bf16[3,24,1280]{2,1,0:T(8,128)(2,1)}), bf16[3,24,1280]{2,1,0:T(8,128)(2,1)S(1)}, u32[]{:S(2)}, u32[]{:S(2)}) async-start(bf16[3,24,1280]{2,1,0:T(8,128)(2,1)} %broadcast_in_dim.4), calls=%async_computation | async-start | bytes 368640 | tf_op jit(solution)/shard_map/all_to_all | solution.py:23
  22.0 14.0 %copy-start.2 = (bf16[3,24,1280]{2,1,0:T(8,128)(2,1)}, bf16[3,24,1280]{2,1,0:T(8,128)(2,1)S(1)}, u32[]{:S(2)}) copy-start(bf16[3,24,1280]{2,1,0:T(8,128)(2,1)S(1)} %all-to-all-done) | copy-start | bytes 552964
  23.0 45.7 %all-to-all-start.1 = ((bf16[16,24,1152]{2,1,0:T(8,128)(2,1)}), bf16[16,24,1152]{2,1,0:T(8,128)(2,1)S(1)}, u32[]{:S(2)}, u32[]{:S(2)}) async-start(bf16[16,24,1152]{2,1,0:T(8,128)(2,1)} %broadcast_in_dim.5), calls=%async_computation.1 | async-start | bytes 1769472 | tf_op jit(solution)/shard_map/all_to_all | solution.py:23
  36.0 50.4 %all-gather.2.cloned.1.call-start = ((), (), s32[]{:S(2)}) async-start(), calls=%async_computation.4 | async-start | bytes 1658880 | tf_op jit(solution)/shard_map/all_gather | solution.py:44
  68.7 18.9 %collective-permute-start = (bf16[384,1152]{1,0:T(8,128)(2,1)S(1)}, bf16[384,1152]{1,0:T(8,128)(2,1)S(1)}, u32[]{:S(2)}, u32[]{:S(2)}) collective-permute-start(bf16[384,1152]{1,0:T(8,128)(2,1)S(1)} %bitcast.20), channel_id=1, source_target_pairs={{0,24},{24,0},{1,25},{25,1},{2,26},{26,2},{3,27},{27,3},{4,28},{28... | collective-permute-start | bytes 2654216 | tf_op jit(solution)/shard_map/ppermute | solution.py:46
  87.6 2.4 %copy-start.3 = (bf16[576,1280]{1,0:T(8,128)(2,1)S(1)}, bf16[576,1280]{1,0:T(8,128)(2,1)}, u32[]{:S(2)}) copy-start(bf16[576,1280]{1,0:T(8,128)(2,1)} %all-gather.2.cloned.1.call-done) | copy-start | bytes 4423684
  91.0 4.3 %collective-permute-start.1 = (bf16[384,1152]{1,0:T(8,128)(2,1)S(1)}, bf16[384,1152]{1,0:T(8,128)(2,1)S(1)}, u32[]{:S(2)}, u32[]{:S(2)}) collective-permute-start(bf16[384,1152]{1,0:T(8,128)(2,1)S(1)} %fusion.2), channel_id=1, source_target_pairs={{0,24},{24,0},{1,25},{25,1},{2,26},{26,2},{3,27},{27,3},{4,28},{28... | collective-permute-start | bytes 2654216 | tf_op jit(solution)/shard_map/ppermute | solution.py:70
  97.2 45.9 %all-to-all-start.3 = ((bf16[16,24,1152]{2,1,0:T(8,128)(2,1)}), bf16[16,24,1152]{2,1,0:T(8,128)(2,1)S(1)}, u32[]{:S(2)}, u32[]{:S(2)}) async-start(bf16[16,24,1152]{2,1,0:T(8,128)(2,1)} %bitcast.7), calls=%async_computation.3 | async-start | bytes 1769472 | tf_op jit(solution)/shard_map/all_to_all | solution.py:23
  143.1 7.3 %copy-start = (bf16[24,1152]{1,0:T(8,128)(2,1)S(1)}, bf16[24,1152]{1,0:T(8,128)(2,1)}, u32[]{:S(2)}) copy-start(bf16[24,1152]{1,0:T(8,128)(2,1)} %param.6) | copy-start | bytes 165892
  143.1 44.5 %all-to-all-start.2 = ((bf16[24,24,1152]{2,1,0:T(8,128)(2,1)}), bf16[24,24,1152]{2,1,0:T(8,128)(2,1)S(1)}, u32[]{:S(2)}, u32[]{:S(2)}) async-start(bf16[24,24,1152]{2,1,0:T(8,128)(2,1)} %bitcast.6), calls=%async_computation.2 | async-start | bytes 2654208 | tf_op jit(solution)/shard_map/all_to_all | solution.py:23
  150.3 37.5 %copy-start.1 = (bf16[24,1152]{1,0:T(8,128)(2,1)S(1)}, bf16[24,1152]{1,0:T(8,128)(2,1)}, u32[]{:S(2)}) copy-start(bf16[24,1152]{1,0:T(8,128)(2,1)} %param.5) | copy-start | bytes 165892
Sparse Core Ops, SparseCore 0:
  39.2 47.1 all-gather.1

commit v2 on v1

v2 whole, which is shorter than its diff:
```python
import jax
import jax.numpy as jnp
from jax import lax
from jax.sharding import Mesh, PartitionSpec as P

EPS = 1e-06
BF = jnp.bfloat16
F32 = jnp.float32
STEPS = (("zh", 2), ("zh", 1), ("x", 2), ("x", 1), ("c", 1))


def normalize(raw):
    wide = raw.astype(F32)
    inverse = lax.rsqrt(jnp.sum(wide * wide, axis=-1, keepdims=True) + EPS)
    return (wide * inverse, inverse)


def project_back(hat, inverse, dnorm):
    return (dnorm - hat * jnp.sum(hat * dnorm, axis=-1, keepdims=True)) * inverse


def exchange(blocks, axes):
    return lax.all_to_all(blocks, axes, split_axis=0, concat_axis=0, tiled=True)


def spread(block, axis):
    count = lax.axis_size(axis)
    copies = jnp.broadcast_to(block[None], (count,) + block.shape)
    return exchange(copies, axis).reshape(count * block.shape[0], block.shape[1])


def gather_sum(part, axis):
    count = lax.axis_size(axis)
    blocks = part.astype(BF).reshape(count, part.shape[0] // count, part.shape[1])
    return jnp.sum(exchange(blocks, axis).astype(F32), axis=0)


def partner(x, axis, bit):
    return lax.ppermute(x, axis, [(i, i ^ bit) for i in range(lax.axis_size(axis))])


def on_device(img_raw, txt_raw, labels, log_logit_scale, bias):
    blk, width = img_raw.shape
    n_x, n_c, n_zl, n_y = (lax.axis_size(a) for a in ("x", "c", "zl", "y"))
    temperature = jnp.exp(log_logit_scale[0])
    shift = bias[0]
    img_hat, img_inv = normalize(img_raw)
    txt_hat, txt_inv = normalize(txt_raw)

    high = labels // 256
    tail = jnp.stack([high, labels - 256 * high], axis=1).astype(BF)
    tail = jnp.pad(tail, ((0, 0), (0, 126)))
    packed = jnp.concatenate([img_hat.astype(BF), tail], axis=1)
    packed = spread(packed, "zl")

    txt = txt_hat.astype(BF)
    owner = jnp.zeros((1,), jnp.int32)
    for step, (axis, bit) in enumerate(STEPS):
        weight = bit * {"zh": n_x * n_c, "x": n_c, "c": 1}[axis]
        txt = jnp.concatenate([txt, partner(txt, axis, bit)], axis=0)
        owner = jnp.concatenate([owner, owner ^ weight])
        if step == 0:
            txt, packed = lax.optimization_barrier((txt, packed))
            packed = spread(packed, "y")
    n_row = owner.shape[0]
    half = n_row // 2 * blk

    img = packed[:, :width]
    marks = packed[:, width : width + 2].astype(F32)
    target = (marks[:, :1] * 256.0 + marks[:, 1:]).astype(jnp.int32)

    me = (lax.axis_index("zh") * n_x + lax.axis_index("x")) * n_c + lax.axis_index("c")
    first = (lax.axis_index("zl") * n_y + lax.axis_index("y")) * n_row
    columns = (first + (owner ^ me))[:, None] * blk + jnp.arange(blk, dtype=jnp.int32)[None, :]
    scores = lax.dot_general(img, txt, (((1,), (1,)), ((), ())), preferred_element_type=F32)
    positive = (target == columns.reshape(1, -1)).astype(F32)
    grad = (jax.nn.sigmoid(temperature * scores + shift) - positive).astype(BF)

    def txt_part(part):
        return lax.dot_general(part, img, (((0,), (0,)), ((), ())), preferred_element_type=F32)

    arrived = partner(txt_part(grad[:, half:]).astype(BF), *STEPS[-1])
    txt_sum = txt_part(grad[:, :half]) + arrived.astype(F32)
    for axis, bit in STEPS[-2::-1]:
        half = txt_sum.shape[0] // 2
        arrived = partner(txt_sum[half:].astype(BF), axis, bit)
        txt_sum = txt_sum[:half] + arrived.astype(F32)

    img_sum = jnp.dot(grad, txt, preferred_element_type=F32)
    img_sum = gather_sum(gather_sum(img_sum, "y"), "zl")

    return (
        project_back(img_hat, img_inv, temperature * img_sum),
        project_back(txt_hat, txt_inv, temperature * txt_sum),
    )


def solution(mesh):
    fine = Mesh(mesh.devices.reshape(4, 4, 2, 3, 8), ("zh", "x", "c", "zl", "y"))
    row, col = ("zh", "x", "c"), ("zl", "y")
    return jax.shard_map(
        on_device,
        mesh=fine,
        in_specs=(P(row + col, None), P(col + row, None), P(row + col), P(), P()),
        out_specs=(P(row + col, None), P(col + row, None)),
        check_vma=False,
    )
```

time: 196 us -> 153 us (0.78)
  the two profiles are of different devices: /device:TPU:256 before, /device:TPU:6 now
where the time goes in v2:
time: 153 us; the launch traced here: 152 us
  starting transfers between devices  71.7 us (47%)
  waiting for transfers between devices  51.9 us (34%)
  other arithmetic  9.43 us (6%)
  matrix products  8.75 us (6%)
  local copies, waits for them, and re-layouts  8.07 us (5%)
  between operations  2.24 us (1%)
    ppermute x10, starting transfers between devices, partner(): lax.ppermute(x, axis, [(i, i ^ bit) for i in range(lax.axis_size(axis))])  51.5 us
    ppermute x10, waiting for transfers between devices, partner(): lax.ppermute(x, axis, [(i, i ^ bit) for i in range(lax.axis_size(axis))])  37.2 us
    all_to_all x4, starting transfers between devices, exchange(): return lax.all_to_all(blocks, axes, split_axis=0, concat_axis=0, tiled=True)  20.2 us
    all_to_all x4, waiting for transfers between devices, exchange(): return lax.all_to_all(blocks, axes, split_axis=0, concat_axis=0, tiled=True)  14.7 us
    unnamed x14, local copies, waits for them, and re-layouts  4.08 us
    dot_general x1, matrix products, on_device(): img_sum = jnp.dot(grad, txt, preferred_element_type=F32)  3.89 us
  transfers between devices with their start and end apart: 14, of which 11 were waited for; matrix products, arithmetic and copies ran while one was open for 9% of the time, Pallas kernels for 0%

profile of v2, /device:TPU:6, one launch (start us, length us, event | category | flops | bytes accessed | tf_op | source)
XLA Modules:
  0.0 152.2 jit_solution(4790377987130362482)
XLA Ops:
  4.6 5.5 %all-to-all-start = ((bf16[3,24,1280]{2,1,0:T(8,128)(2,1)}), bf16[3,24,1280]{2,1,0:T(8,128)(2,1)S(1)}, u32[]{:S(2)}, u32[]{:S(2)}) async-start(bf16[3,24,1280]{2,1,0:T(8,128)(2,1)} %broadcast_in_dim.4), calls=%async_computation | async-start | bytes 368640 | tf_op jit(solution)/shard_map/all_to_all | solution.py:23
  11.9 13.9 %collective-permute-start = (bf16[24,1152]{1,0:T(8,128)(2,1)S(1)}, bf16[24,1152]{1,0:T(8,128)(2,1)S(1)}, u32[]{:S(2)}, u32[]{:S(2)}) collective-permute-start(bf16[24,1152]{1,0:T(8,128)(2,1)S(1)} %fusion.15), channel_id=1, source_target_pairs={{0,384},{192,576},{384,0},{576,192},{1,385},{193,577},{385,1},{577... | collective-permute-start | bytes 165896 | tf_op jit(solution)/shard_map/ppermute | solution.py:39
  25.8 3.4 %collective-permute-done = bf16[24,1152]{1,0:T(8,128)(2,1)S(1)} collective-permute-done((bf16[24,1152]{1,0:T(8,128)(2,1)S(1)}, bf16[24,1152]{1,0:T(8,128)(2,1)S(1)}, u32[]{:S(2)}, u32[]{:S(2)}) %collective-permute-start) | collective-permute-done | bytes 55328 | tf_op jit(solution)/shard_map/ppermute | solution.py:39
  29.2 4.2 %collective-permute-start.1 = (bf16[48,1152]{1,0:T(8,128)(2,1)S(1)}, bf16[48,1152]{1,0:T(8,128)(2,1)S(1)}, u32[]{:S(2)}, u32[]{:S(2)}) collective-permute-start(bf16[48,1152]{1,0:T(8,128)(2,1)S(1)} %pad_maximum_fusion.3), channel_id=1, source_target_pairs={{0,192},{192,0},{384,576},{576,384},{1,193},{193,1},{385,577},{577... | collective-permute-start | bytes 331784 | tf_op jit(solution)/shard_map/ppermute | solution.py:39
  34.6 7.2 %all-to-all-start.1 = ((bf16[8,72,1280]{2,1,0:T(8,128)(2,1)}), bf16[8,72,1280]{2,1,0:T(8,128)(2,1)S(1)}, u32[]{:S(2)}, u32[]{:S(2)}) async-start(bf16[8,72,1280]{2,1,0:T(8,128)(2,1)} %broadcast_in_dim.5), calls=%async_computation.1 | async-start | bytes 2949120 | tf_op jit(solution)/shard_map/all_to_all | solution.py:23
  42.4 3.3 %collective-permute-start.2 = (bf16[96,1152]{1,0:T(8,128)(2,1)S(1)}, bf16[96,1152]{1,0:T(8,128)(2,1)S(1)}, u32[]{:S(2)}, u32[]{:S(2)}) collective-permute-start(bf16[96,1152]{1,0:T(8,128)(2,1)S(1)} %pad_maximum_fusion.2), channel_id=1, source_target_pairs={{0,96},{48,144},{96,0},{144,48},{1,97},{49,145},{97,1},{145,49},{2... | collective-permute-start | bytes 663560 | tf_op jit(solution)/shard_map/ppermute | solution.py:39
  45.8 6.0 %collective-permute-done.2 = bf16[96,1152]{1,0:T(8,128)(2,1)S(1)} collective-permute-done((bf16[96,1152]{1,0:T(8,128)(2,1)S(1)}, bf16[96,1152]{1,0:T(8,128)(2,1)S(1)}, u32[]{:S(2)}, u32[]{:S(2)}) %collective-permute-start.2) | collective-permute-done | bytes 221216 | tf_op jit(solution)/shard_map/ppermute | solution.py:39
  51.8 2.7 %collective-permute-start.3 = (bf16[192,1152]{1,0:T(8,128)(2,1)S(1)}, bf16[192,1152]{1,0:T(8,128)(2,1)S(1)}, u32[]{:S(2)}, u32[]{:S(2)}) collective-permute-start(bf16[192,1152]{1,0:T(8,128)(2,1)S(1)} %pad_maximum_fusion.1), channel_id=1, source_target_pairs={{0,48},{48,0},{96,144},{144,96},{1,49},{49,1},{97,145},{145,97},{2... | collective-permute-start | bytes 1327112 | tf_op jit(solution)/shard_map/ppermute | solution.py:39
  56.1 5.9 %collective-permute-done.3 = bf16[192,1152]{1,0:T(8,128)(2,1)S(1)} collective-permute-done((bf16[192,1152]{1,0:T(8,128)(2,1)S(1)}, bf16[192,1152]{1,0:T(8,128)(2,1)S(1)}, u32[]{:S(2)}, u32[]{:S(2)}) %collective-permute-start.3) | collective-permute-done | bytes 442400 | tf_op jit(solution)/shard_map/ppermute | solution.py:39
  67.8 10.2 %all-to-all-done.1 = bf16[8,72,1280]{2,1,0:T(8,128)(2,1)S(1)} async-done(((bf16[8,72,1280]{2,1,0:T(8,128)(2,1)}), bf16[8,72,1280]{2,1,0:T(8,128)(2,1)S(1)}, u32[]{:S(2)}, u32[]{:S(2)}) %all-to-all-start.1) | async-done | bytes 1474592 | tf_op jit(solution)/shard_map/all_to_all | solution.py:23
  78.3 3.0 %subtract_convert_fusion = bf16[576,768]{1,0:T(8,128)(2,1)S(1)} fusion(bf16[768,1152]{1,0:T(8,128)(2,1)} %constant_dynamic-update-slice_fusion, bf16[576,1280]{1,0:T(8,128)(2,1)S(1)} %bitcast.15, s32[768]{0:T(1024)S(1)} %add.99, f32[]{:T(128)} %bitcast.13, f32[]{:T(128)} %bitcast, s32[576]{0:T(1024)S(1)} %fusion.9), kind=kOutput, calls=%fused_computation.3 | convolution fusion | flops 1023197184 | bytes 3989512 | tf_op jit(solution)/shard_map/dot_general | solution.py:75
  84.2 2.4 %collective-permute-done.5 = bf16[384,1152]{1,0:T(8,128)(2,1)S(1)} collective-permute-done((bf16[384,1152]{1,0:T(8,128)(2,1)S(1)}, bf16[384,1152]{1,0:T(8,128)(2,1)S(1)}, u32[]{:S(2)}, u32[]{:S(2)}) %collective-permute-start.5) | collective-permute-done | bytes 884768 | tf_op jit(solution)/shard_map/ppermute | solution.py:39
  89.6 2.7 %collective-permute-start.6 = (bf16[192,1152]{1,0:T(8,128)(2,1)}, bf16[192,1152]{1,0:T(8,128)(2,1)}, u32[]{:S(2)}, u32[]{:S(2)}) collective-permute-start(bf16[192,1152]{1,0:T(8,128)(2,1)} %slice.109), channel_id=1, source_target_pairs={{0,48},{48,0},{96,144},{144,96},{1,49},{49,1},{97,145},{145,97},{2... | collective-permute-start | bytes 1327112 | tf_op jit(solution)/shard_map/ppermute | solution.py:39
  92.3 3.9 %convolution_convert_fusion = bf16[576,1152]{1,0:T(8,128)(2,1)} fusion(bf16[576,768]{1,0:T(8,128)(2,1)S(1)} %subtract_convert_fusion, bf16[768,1152]{1,0:T(8,128)(2,1)} %constant_dynamic-update-slice_fusion), kind=kOutput, calls=%fused_computation | convolution fusion | flops 1019879424 | bytes 3981312 | tf_op jit(solution)/shard_map/dot_general | solution.py:89
  96.2 3.7 %all-to-all-start.2 = ((bf16[8,72,1152]{2,1,0:T(8,128)(2,1)}), bf16[8,72,1152]{2,1,0:T(8,128)(2,1)S(1)}, u32[]{:S(2)}, u32[]{:S(2)}) async-start(bf16[8,72,1152]{2,1,0:T(8,128)(2,1)} %bitcast.6), calls=%async_computation.2 | async-start | bytes 2654208 | tf_op jit(solution)/shard_map/all_to_all | solution.py:23
  99.9 4.1 %collective-permute-done.6 = bf16[192,1152]{1,0:T(8,128)(2,1)} collective-permute-done((bf16[192,1152]{1,0:T(8,128)(2,1)}, bf16[192,1152]{1,0:T(8,128)(2,1)}, u32[]{:S(2)}, u32[]{:S(2)}) %collective-permute-start.6) | collective-permute-done | bytes 442400 | tf_op jit(solution)/shard_map/ppermute | solution.py:39
  105.1 3.3 %collective-permute-start.7 = (bf16[96,1152]{1,0:T(8,128)(2,1)S(1)}, bf16[96,1152]{1,0:T(8,128)(2,1)S(1)}, u32[]{:S(2)}, u32[]{:S(2)}) collective-permute-start(bf16[96,1152]{1,0:T(8,128)(2,1)S(1)} %slice.110), channel_id=1, source_target_pairs={{0,96},{48,144},{96,0},{144,48},{1,97},{49,145},{97,1},{145,49},{2... | collective-permute-start | bytes 663560 | tf_op jit(solution)/shard_map/ppermute | solution.py:39
  108.4 6.7 %collective-permute-done.7 = bf16[96,1152]{1,0:T(8,128)(2,1)S(1)} collective-permute-done((bf16[96,1152]{1,0:T(8,128)(2,1)S(1)}, bf16[96,1152]{1,0:T(8,128)(2,1)S(1)}, u32[]{:S(2)}, u32[]{:S(2)}) %collective-permute-start.7) | collective-permute-done | bytes 221216 | tf_op jit(solution)/shard_map/ppermute | solution.py:39
  115.2 2.6 %collective-permute-start.8 = (bf16[48,1152]{1,0:T(8,128)(2,1)S(1)}, bf16[48,1152]{1,0:T(8,128)(2,1)S(1)}, u32[]{:S(2)}, u32[]{:S(2)}) collective-permute-start(bf16[48,1152]{1,0:T(8,128)(2,1)S(1)} %slice.111), channel_id=1, source_target_pairs={{0,192},{192,0},{384,576},{576,384},{1,193},{193,1},{385,577},{577... | collective-permute-start | bytes 331784 | tf_op jit(solution)/shard_map/ppermute | solution.py:39
  117.8 5.8 %collective-permute-done.8 = bf16[48,1152]{1,0:T(8,128)(2,1)S(1)} collective-permute-done((bf16[48,1152]{1,0:T(8,128)(2,1)S(1)}, bf16[48,1152]{1,0:T(8,128)(2,1)S(1)}, u32[]{:S(2)}, u32[]{:S(2)}) %collective-permute-start.8) | collective-permute-done | bytes 110624 | tf_op jit(solution)/shard_map/ppermute | solution.py:39
  123.7 14.9 %collective-permute-start.9 = (bf16[24,1152]{1,0:T(8,128)(2,1)S(1)}, bf16[24,1152]{1,0:T(8,128)(2,1)S(1)}, u32[]{:S(2)}, u32[]{:S(2)}) collective-permute-start(bf16[24,1152]{1,0:T(8,128)(2,1)S(1)} %slice.112), channel_id=1, source_target_pairs={{0,384},{192,576},{384,0},{576,192},{1,385},{193,577},{385,1},{577... | collective-permute-start | bytes 165896 | tf_op jit(solution)/shard_map/ppermute | solution.py:39
  138.6 2.4 %collective-permute-done.9 = bf16[24,1152]{1,0:T(8,128)(2,1)S(1)} collective-permute-done((bf16[24,1152]{1,0:T(8,128)(2,1)S(1)}, bf16[24,1152]{1,0:T(8,128)(2,1)S(1)}, u32[]{:S(2)}, u32[]{:S(2)}) %collective-permute-start.9) | collective-permute-done | bytes 55328 | tf_op jit(solution)/shard_map/ppermute | solution.py:39
  142.1 3.9 %all-to-all-start.3 = ((bf16[3,24,1152]{2,1,0:T(8,128)(2,1)}), bf16[3,24,1152]{2,1,0:T(8,128)(2,1)S(1)}, u32[]{:S(2)}, u32[]{:S(2)}) async-start(bf16[3,24,1152]{2,1,0:T(8,128)(2,1)} %bitcast.7), calls=%async_computation.3 | async-start | bytes 331776 | tf_op jit(solution)/shard_map/all_to_all | solution.py:23
  146.7 4.5 %all-to-all-done.3 = bf16[3,24,1152]{2,1,0:T(8,128)(2,1)S(1)} async-done(((bf16[3,24,1152]{2,1,0:T(8,128)(2,1)}), bf16[3,24,1152]{2,1,0:T(8,128)(2,1)S(1)}, u32[]{:S(2)}, u32[]{:S(2)}) %all-to-all-start.3) | async-done | bytes 165920 | tf_op jit(solution)/shard_map/all_to_all | solution.py:23
  (58 shorter events, 23.8 us)
Async XLA Ops:
  4.6 24.6 %all-to-all-start = ((bf16[3,24,1280]{2,1,0:T(8,128)(2,1)}), bf16[3,24,1280]{2,1,0:T(8,128)(2,1)S(1)}, u32[]{:S(2)}, u32[]{:S(2)}) async-start(bf16[3,24,1280]{2,1,0:T(8,128)(2,1)} %broadcast_in_dim.4), calls=%async_computation | async-start | bytes 368640 | tf_op jit(solution)/shard_map/all_to_all | solution.py:23
  11.9 17.3 %collective-permute-start = (bf16[24,1152]{1,0:T(8,128)(2,1)S(1)}, bf16[24,1152]{1,0:T(8,128)(2,1)S(1)}, u32[]{:S(2)}, u32[]{:S(2)}) collective-permute-start(bf16[24,1152]{1,0:T(8,128)(2,1)S(1)} %fusion.15), channel_id=1, source_target_pairs={{0,384},{192,576},{384,0},{576,192},{1,385},{193,577},{385,1},{577... | collective-permute-start | bytes 165896 | tf_op jit(solution)/shard_map/ppermute | solution.py:39
  29.2 13.2 %collective-permute-start.1 = (bf16[48,1152]{1,0:T(8,128)(2,1)S(1)}, bf16[48,1152]{1,0:T(8,128)(2,1)S(1)}, u32[]{:S(2)}, u32[]{:S(2)}) collective-permute-start(bf16[48,1152]{1,0:T(8,128)(2,1)S(1)} %pad_maximum_fusion.3), channel_id=1, source_target_pairs={{0,192},{192,0},{384,576},{576,384},{1,193},{193,1},{385,577},{577... | collective-permute-start | bytes 331784 | tf_op jit(solution)/shard_map/ppermute | solution.py:39
  34.6 19.9 %copy-start.4 = (s32[32]{0:T(128)S(1)}, s32[32]{0:T(128)}, u32[]{:S(2)}) copy-start(s32[32]{0:T(128)} %constant.62.clone.1) | copy-start | bytes 388
  34.6 43.4 %all-to-all-start.1 = ((bf16[8,72,1280]{2,1,0:T(8,128)(2,1)}), bf16[8,72,1280]{2,1,0:T(8,128)(2,1)S(1)}, u32[]{:S(2)}, u32[]{:S(2)}) async-start(bf16[8,72,1280]{2,1,0:T(8,128)(2,1)} %broadcast_in_dim.5), calls=%async_computation.1 | async-start | bytes 2949120 | tf_op jit(solution)/shard_map/all_to_all | solution.py:23
  42.4 9.3 %collective-permute-start.2 = (bf16[96,1152]{1,0:T(8,128)(2,1)S(1)}, bf16[96,1152]{1,0:T(8,128)(2,1)S(1)}, u32[]{:S(2)}, u32[]{:S(2)}) collective-permute-start(bf16[96,1152]{1,0:T(8,128)(2,1)S(1)} %pad_maximum_fusion.2), channel_id=1, source_target_pairs={{0,96},{48,144},{96,0},{144,48},{1,97},{49,145},{97,1},{145,49},{2... | collective-permute-start | bytes 663560 | tf_op jit(solution)/shard_map/ppermute | solution.py:39
  51.8 10.2 %collective-permute-start.3 = (bf16[192,1152]{1,0:T(8,128)(2,1)S(1)}, bf16[192,1152]{1,0:T(8,128)(2,1)S(1)}, u32[]{:S(2)}, u32[]{:S(2)}) collective-permute-start(bf16[192,1152]{1,0:T(8,128)(2,1)S(1)} %pad_maximum_fusion.1), channel_id=1, source_target_pairs={{0,48},{48,0},{96,144},{144,96},{1,49},{49,1},{97,145},{145,97},{2... | collective-permute-start | bytes 1327112 | tf_op jit(solution)/shard_map/ppermute | solution.py:39
  62.1 4.8 %collective-permute-start.4 = (bf16[384,1152]{1,0:T(8,128)(2,1)S(1)}, bf16[384,1152]{1,0:T(8,128)(2,1)S(1)}, u32[]{:S(2)}, u32[]{:S(2)}) collective-permute-start(bf16[384,1152]{1,0:T(8,128)(2,1)S(1)} %pad_maximum_fusion), channel_id=1, source_target_pairs={{0,24},{24,0},{1,25},{25,1},{2,26},{26,2},{3,27},{27,3},{4,28},{28... | collective-permute-start | bytes 2654216 | tf_op jit(solution)/shard_map/ppermute | solution.py:39
  82.2 4.3 %collective-permute-start.5 = (bf16[384,1152]{1,0:T(8,128)(2,1)S(1)}, bf16[384,1152]{1,0:T(8,128)(2,1)S(1)}, u32[]{:S(2)}, u32[]{:S(2)}) collective-permute-start(bf16[384,1152]{1,0:T(8,128)(2,1)S(1)} %convolution_convert_fusion.1), channel_id=1, source_target_pairs={{0,24},{24,0},{1,25},{25,1},{2,26},{26,2},{3,27},{27,3},{4,28},{28... | collective-permute-start | bytes 2654216 | tf_op jit(solution)/shard_map/ppermute | solution.py:39
  87.5 1.2 copy-start
  89.6 14.4 %collective-permute-start.6 = (bf16[192,1152]{1,0:T(8,128)(2,1)}, bf16[192,1152]{1,0:T(8,128)(2,1)}, u32[]{:S(2)}, u32[]{:S(2)}) collective-permute-start(bf16[192,1152]{1,0:T(8,128)(2,1)} %slice.109), channel_id=1, source_target_pairs={{0,48},{48,0},{96,144},{144,96},{1,49},{49,1},{97,145},{145,97},{2... | collective-permute-start | bytes 1327112 | tf_op jit(solution)/shard_map/ppermute | solution.py:39
  96.2 7.8 %copy-start.1 = (f32[384,1152]{1,0:T(8,128)S(1)}, f32[384,1152]{1,0:T(8,128)}, u32[]{:S(2)}) copy-start(f32[384,1152]{1,0:T(8,128)} %copy-done) | copy-start | bytes 5308420
  96.2 45.0 %all-to-all-start.2 = ((bf16[8,72,1152]{2,1,0:T(8,128)(2,1)}), bf16[8,72,1152]{2,1,0:T(8,128)(2,1)S(1)}, u32[]{:S(2)}, u32[]{:S(2)}) async-start(bf16[8,72,1152]{2,1,0:T(8,128)(2,1)} %bitcast.6), calls=%async_computation.2 | async-start | bytes 2654208 | tf_op jit(solution)/shard_map/all_to_all | solution.py:23
  99.9 41.1 %copy-start.2 = (bf16[24,1152]{1,0:T(8,128)(2,1)S(1)}, bf16[24,1152]{1,0:T(8,128)(2,1)}, u32[]{:S(2)}) copy-start(bf16[24,1152]{1,0:T(8,128)(2,1)} %param.6) | copy-start | bytes 165892
  105.1 10.0 %collective-permute-start.7 = (bf16[96,1152]{1,0:T(8,128)(2,1)S(1)}, bf16[96,1152]{1,0:T(8,128)(2,1)S(1)}, u32[]{:S(2)}, u32[]{:S(2)}) collective-permute-start(bf16[96,1152]{1,0:T(8,128)(2,1)S(1)} %slice.110), channel_id=1, source_target_pairs={{0,96},{48,144},{96,0},{144,48},{1,97},{49,145},{97,1},{145,49},{2... | collective-permute-start | bytes 663560 | tf_op jit(solution)/shard_map/ppermute | solution.py:39
  115.2 36.0 %copy-start.3 = (bf16[24,1152]{1,0:T(8,128)(2,1)S(1)}, bf16[24,1152]{1,0:T(8,128)(2,1)}, u32[]{:S(2)}) copy-start(bf16[24,1152]{1,0:T(8,128)(2,1)} %param.5) | copy-start | bytes 165892
  115.2 8.4 %collective-permute-start.8 = (bf16[48,1152]{1,0:T(8,128)(2,1)S(1)}, bf16[48,1152]{1,0:T(8,128)(2,1)S(1)}, u32[]{:S(2)}, u32[]{:S(2)}) collective-permute-start(bf16[48,1152]{1,0:T(8,128)(2,1)S(1)} %slice.111), channel_id=1, source_target_pairs={{0,192},{192,0},{384,576},{576,384},{1,193},{193,1},{385,577},{577... | collective-permute-start | bytes 331784 | tf_op jit(solution)/shard_map/ppermute | solution.py:39
  123.7 17.3 %collective-permute-start.9 = (bf16[24,1152]{1,0:T(8,128)(2,1)S(1)}, bf16[24,1152]{1,0:T(8,128)(2,1)S(1)}, u32[]{:S(2)}, u32[]{:S(2)}) collective-permute-start(bf16[24,1152]{1,0:T(8,128)(2,1)S(1)} %slice.112), channel_id=1, source_target_pairs={{0,384},{192,576},{384,0},{576,192},{1,385},{193,577},{385,1},{577... | collective-permute-start | bytes 165896 | tf_op jit(solution)/shard_map/ppermute | solution.py:39
  142.1 9.1 %all-to-all-start.3 = ((bf16[3,24,1152]{2,1,0:T(8,128)(2,1)}), bf16[3,24,1152]{2,1,0:T(8,128)(2,1)S(1)}, u32[]{:S(2)}, u32[]{:S(2)}) async-start(bf16[3,24,1152]{2,1,0:T(8,128)(2,1)} %bitcast.7), calls=%async_computation.3 | async-start | bytes 331776 | tf_op jit(solution)/shard_map/all_to_all | solution.py:23

commit v3 on v2

v3 whole, which is shorter than its diff:
```python
import jax
import jax.numpy as jnp
from jax import lax
from jax.experimental import pallas as pl
from jax.experimental.pallas import tpu as pltpu
from jax.sharding import Mesh, PartitionSpec as P

EPS = 1e-06
BF = jnp.bfloat16
F32 = jnp.float32
Z = ("zh", "zl")
RUN = 4


def normalize(raw):
    wide = raw.astype(F32)
    inverse = lax.rsqrt(jnp.sum(wide * wide, axis=-1, keepdims=True) + EPS)
    return (wide * inverse, inverse)


def prepare(img_ref, txt_ref, label_ref, packed_ref, copies_ref, img_inv_ref, txt_inv_ref):
    blk, width = img_ref.shape
    img_hat, img_inv_ref[...] = normalize(img_ref[...])
    packed_ref[:, :width] = img_hat.astype(BF)
    row = lax.broadcasted_iota(jnp.int32, (blk, blk), 0)
    lane = lax.broadcasted_iota(jnp.int32, (blk, blk), 1)
    spot = jnp.where(row == lane, label_ref[...].astype(F32), 0.0)
    label = jnp.sum(spot, axis=1, keepdims=True).astype(jnp.int32)
    high = label >> 8
    place = lax.broadcasted_iota(jnp.int32, (blk, packed_ref.shape[1] - width), 1)
    tail = jnp.where(place == 0, high, jnp.where(place == 1, label - 256 * high, 0))
    packed_ref[:, width:] = tail.astype(F32).astype(BF)
    txt_hat, txt_inv_ref[...] = normalize(txt_ref[...])
    txt = txt_hat.astype(BF)
    for i in range(copies_ref.shape[0]):
        copies_ref[i] = txt


def project_back(raw, inverse, dnorm):
    hat = raw.astype(F32) * inverse
    return (dnorm - hat * jnp.sum(hat * dnorm, axis=-1, keepdims=True)) * inverse


def exchange(blocks, axes):
    groups = None
    if axes == Z:
        groups = [list(range(i, i + RUN)) for i in range(0, lax.axis_size(Z), RUN)]
    return lax.all_to_all(
        blocks, axes, split_axis=0, concat_axis=0, axis_index_groups=groups, tiled=True
    )


def spread(block, axes, count):
    copies = jnp.broadcast_to(block[None], (count,) + block.shape)
    return joined(exchange(copies, axes))


def joined(blocks):
    return blocks.reshape(-1, blocks.shape[-1])


def scattered(part, axes, count):
    blocks = part.astype(BF).reshape(count, part.shape[0] // count, part.shape[1])
    return exchange(blocks, axes)


def send(x, axis, hop):
    size = lax.axis_size(axis)
    return lax.ppermute(x.astype(BF), axis, [(i, (i + hop) % size) for i in range(size)])


def on_device(img_raw, txt_raw, labels, log_logit_scale, bias):
    blk, width = img_raw.shape
    n_z, n_zl, n_x, n_c, n_y = (lax.axis_size(a) for a in (Z, "zl", "x", "c", "y"))
    temperature = jnp.exp(log_logit_scale[0])
    shift = bias[0]
    vmem = pl.BlockSpec(memory_space=pltpu.VMEM)
    packed, txt, img_inv, txt_inv = pl.pallas_call(
        prepare,
        out_shape=[
            jax.ShapeDtypeStruct((blk, width + 128), BF),
            jax.ShapeDtypeStruct((RUN, blk, width), BF),
            jax.ShapeDtypeStruct((blk, 1), F32),
            jax.ShapeDtypeStruct((blk, 1), F32),
        ],
        in_specs=[vmem] * 3,
        out_specs=[vmem] * 4,
    )(img_raw, txt_raw, labels.reshape(1, blk))

    trio = jnp.concatenate([packed, send(packed, Z, -RUN), send(packed, Z, RUN)])
    trio, txt = lax.optimization_barrier((trio, joined(exchange(txt, Z))))
    wide = jnp.concatenate([send(trio, "y", 3), trio, send(trio, "y", -3)])
    y = trio.shape[0]
    packed = jnp.concatenate([wide, send(wide, "y", -1), send(wide[y:], "y", 1)])
    txt = spread(txt, "x", n_x)
    half = txt.shape[0]
    txt = jnp.concatenate([txt, send(txt, "c", 1)])

    img = packed[:, :width]
    marks = packed[:, width : width + 2].astype(F32)
    target = (marks[:, :1] * 256.0 + marks[:, 1:]).astype(jnp.int32)

    owner = jnp.arange(n_c * n_x * RUN, dtype=jnp.int32)
    at_z = lax.axis_index(Z) // RUN * RUN + owner % RUN
    at_x = owner // RUN % n_x
    at_c = (lax.axis_index("c") + owner // (RUN * n_x)) % n_c
    col = at_z % n_zl * n_y + lax.axis_index("y")
    block = ((col * (n_z // n_zl) + at_z // n_zl) * n_x + at_x) * n_c + at_c
    columns = block[:, None] * blk + jnp.arange(blk, dtype=jnp.int32)[None, :]
    scores = lax.dot_general(img, txt, (((1,), (1,)), ((), ())), preferred_element_type=F32)
    positive = (target == columns.reshape(1, -1)).astype(F32)
    grad = (jax.nn.sigmoid(temperature * scores + shift) - positive).astype(BF)

    def txt_part(part):
        return lax.dot_general(part, img, (((0,), (0,)), ((), ())), preferred_element_type=F32)

    away = jnp.dot(grad[3 * y :], txt, preferred_element_type=F32).astype(BF)
    away, grad = lax.optimization_barrier((away, grad))
    before, after = send(away[: 3 * y], "y", 1), send(away[3 * y :], "y", -1)

    arrived = send(txt_part(grad[:, half:]), "c", 1)
    txt_sum = txt_part(grad[:, :half]) + arrived.astype(F32)
    txt_sum = jnp.sum(scattered(txt_sum, "x", n_x).astype(F32), axis=0)
    txt_sum = jnp.sum(scattered(txt_sum, Z, RUN).astype(F32), axis=0)

    mine = jnp.dot(grad[: 3 * y], txt, preferred_element_type=F32)
    low = mine[:y] + before[:y].astype(F32)
    mid = mine[y : 2 * y] + before[y : 2 * y].astype(F32) + after[:y].astype(F32)
    top = mine[2 * y :] + before[2 * y :].astype(F32) + after[y:].astype(F32)
    mid = mid + send(low, "y", -3).astype(F32) + send(top, "y", 3).astype(F32)
    one, two = send(mid[blk : 2 * blk], Z, RUN), send(mid[2 * blk :], Z, -RUN)
    img_sum = mid[:blk] + one.astype(F32) + two.astype(F32)
    return (
        project_back(img_raw, img_inv, temperature * img_sum),
        project_back(txt_raw, txt_inv, temperature * txt_sum),
    )


def solution(mesh):
    fine = Mesh(mesh.devices.reshape(4, 4, 2, 3, 8), ("zh", "x", "c", "zl", "y"))
    row, col = ("zh", "x", "c"), ("zl", "y")
    return jax.shard_map(
        on_device,
        mesh=fine,
        in_specs=(P(row + col, None), P(col + row, None), P(row + col), P(), P()),
        out_specs=(P(row + col, None), P(col + row, None)),
        check_vma=False,
    )
```

time: 153 us -> 143 us (0.935)
  waiting for transfers between devices: 51.9 us -> 34.7 us
  starting transfers between devices: 71.7 us -> 81.3 us
  other arithmetic: 9.43 us -> 6.3 us
  local copies, waits for them, and re-layouts: 8.07 us -> 5.55 us
  Pallas kernels: 0 us -> 1.66 us
    ppermute x10 -> x14, waiting for transfers between devices: 37.2 us -> 28.1 us  [send(): lax.ppermute(x.astype(BF), axis, [(i, (i + hop) % size) for i in range(si...]
    ppermute x10 -> x14, starting transfers between devices: 51.5 us -> 60.3 us  [send(): lax.ppermute(x.astype(BF), axis, [(i, (i + hop) % size) for i in range(si...]
    all_to_all x4, waiting for transfers between devices: 14.7 us -> 6.6 us  [exchange(): lax.all_to_all(blocks, axes, split_axis=0, concat_axis=0, axis_index_grou...]
    dot_general x2, matrix products: 1.86 us -> 5.42 us  [txt_part(): lax.dot_general(part, img, (((0,), (0,)), ((), ())), preferred_element_ty...]
    dot_general x1 -> x2, matrix products: 3.89 us -> 1.53 us  [the longest x1 0.91 us: on_device(): away = jnp.dot(grad[3 * y:], txt, preferred_element_type=F32).astype(BF)]
    reduce_sum x4 -> x2, other arithmetic: 2.75 us -> 0.88 us  [the longest x1 0.86 us: on_device(): txt_sum = jnp.sum(scattered(txt_sum, 'x', n_x).astype(F32), axis=0)]
    convert_element_type x2 -> x1, other arithmetic: 1.8 us -> 0.1 us  [send(): x.astype(BF)]
    pallas_call x0 -> x1, Pallas kernels: none -> 1.66 us  [on_device(): pl.pallas_call(prepare, out_shape=[jax.ShapeDtypeStruct((blk, width + 128...]
  transfers between devices with their start and end apart: 14 -> 18, of which waited for: 11 -> 7; matrix products, arithmetic and copies ran while one was open for 9% -> 11% of each run, Pallas kernels for 0% -> 0%
where the time goes in v3:
time: 143 us; the launch traced here: 142 us
  starting transfers between devices  81.3 us (57%)
  waiting for transfers between devices  34.7 us (24%)
  matrix products  9.8 us (7%)
  other arithmetic  6.3 us (4%)
  local copies, waits for them, and re-layouts  5.55 us (4%)
  between operations  2.27 us (2%)
  Pallas kernels  1.66 us (1%)
    ppermute x14, starting transfers between devices, send(): lax.ppermute(x.astype(BF), axis, [(i, (i + hop) % size) for i in range(si...  60.3 us
    ppermute x14, waiting for transfers between devices, send(): lax.ppermute(x.astype(BF), axis, [(i, (i + hop) % size) for i in range(si...  28.1 us
    all_to_all x4, starting transfers between devices, exchange(): lax.all_to_all(blocks, axes, split_axis=0, concat_axis=0, axis_index_grou...  21 us
    all_to_all x4, waiting for transfers between devices, exchange(): lax.all_to_all(blocks, axes, split_axis=0, concat_axis=0, axis_index_grou...  6.6 us
    dot_general x2, matrix products, txt_part(): lax.dot_general(part, img, (((0,), (0,)), ((), ())), preferred_element_ty...  5.42 us
    unnamed x14, local copies, waits for them, and re-layouts  3.64 us
  transfers between devices with their start and end apart: 18, of which 7 were waited for; matrix products, arithmetic and copies ran while one was open for 11% of the time, Pallas kernels for 0%

profile of v3, /device:TPU:6, one launch (start us, length us, event | category | flops | bytes accessed | tf_op | source)
XLA Modules:
  0.0 141.6 jit_solution(14362673267803341055)
XLA Ops:
  2.3 7.3 %all-to-all-start = ((bf16[4,24,1152]{2,1,0:T(8,128)(2,1)}), bf16[4,24,1152]{2,1,0:T(8,128)(2,1)S(1)}, u32[]{:S(2)}, u32[]{:S(2)}) async-start(bf16[4,24,1152]{2,1,0:T(8,128)(2,1)} %get-tuple-element.11), calls=%async_computation | async-start | bytes 442368 | tf_op jit(solution)/shard_map/all_to_all | solution.py:48
  9.5 10.6 %collective-permute-start.1 = (bf16[24,1280]{1,0:T(8,128)(2,1)}, bf16[24,1280]{1,0:T(8,128)(2,1)S(1)}, u32[]{:S(2)}, u32[]{:S(2)}) collective-permute-start(bf16[24,1280]{1,0:T(8,128)(2,1)} %get-tuple-element.10), channel_id=1, source_target_pairs={{0,200},{8,208},{16,384},{192,392},{200,400},{208,576},{384,584},{... | collective-permute-start | bytes 184328 | tf_op jit(solution)/shard_map/ppermute | solution.py:69
  20.2 3.2 %collective-permute-start = (bf16[24,1280]{1,0:T(8,128)(2,1)}, bf16[24,1280]{1,0:T(8,128)(2,1)S(1)}, u32[]{:S(2)}, u32[]{:S(2)}) collective-permute-start(bf16[24,1280]{1,0:T(8,128)(2,1)} %get-tuple-element.10), channel_id=1, source_target_pairs={{0,400},{8,576},{16,584},{192,592},{200,0},{208,8},{384,16},{392,1... | collective-permute-start | bytes 184328 | tf_op jit(solution)/shard_map/ppermute | solution.py:69
  25.1 6.8 %collective-permute-done = bf16[24,1280]{1,0:T(8,128)(2,1)S(1)} collective-permute-done((bf16[24,1280]{1,0:T(8,128)(2,1)}, bf16[24,1280]{1,0:T(8,128)(2,1)S(1)}, u32[]{:S(2)}, u32[]{:S(2)}) %collective-permute-start) | collective-permute-done | bytes 61472 | tf_op jit(solution)/shard_map/ppermute | solution.py:69
  32.8 5.5 %collective-permute-start.2 = (bf16[72,1280]{1,0:T(8,128)(2,1)S(1)}, bf16[72,1280]{1,0:T(8,128)(2,1)S(1)}, u32[]{:S(2)}, u32[]{:S(2)}) collective-permute-start(bf16[72,1280]{1,0:T(8,128)(2,1)S(1)} %pad_maximum_fusion.6), channel_id=1, source_target_pairs={{0,3},{1,4},{2,5},{3,6},{4,7},{5,0},{6,1},{7,2},{8,11},{9,12},{10,... | collective-permute-start | bytes 552968 | tf_op jit(solution)/shard_map/ppermute | solution.py:69
  38.3 3.4 %collective-permute-start.3 = (bf16[72,1280]{1,0:T(8,128)(2,1)S(1)}, bf16[72,1280]{1,0:T(8,128)(2,1)S(1)}, u32[]{:S(2)}, u32[]{:S(2)}) collective-permute-start(bf16[72,1280]{1,0:T(8,128)(2,1)S(1)} %pad_maximum_fusion.6), channel_id=1, source_target_pairs={{0,5},{1,6},{2,7},{3,0},{4,1},{5,2},{6,3},{7,4},{8,13},{9,14},{10,... | collective-permute-start | bytes 552968 | tf_op jit(solution)/shard_map/ppermute | solution.py:69
  44.1 4.8 %all-to-all-start.1 = ((bf16[4,96,1152]{2,1,0:T(8,128)(2,1)}), bf16[4,96,1152]{2,1,0:T(8,128)(2,1)S(1)}, u32[]{:S(2)}, u32[]{:S(2)}) async-start(bf16[4,96,1152]{2,1,0:T(8,128)(2,1)} %broadcast_in_dim.2), calls=%async_computation.1 | async-start | bytes 1769472 | tf_op jit(solution)/shard_map/all_to_all | solution.py:48
  48.9 3.7 %collective-permute-done.3 = bf16[72,1280]{1,0:T(8,128)(2,1)S(1)} collective-permute-done((bf16[72,1280]{1,0:T(8,128)(2,1)S(1)}, bf16[72,1280]{1,0:T(8,128)(2,1)S(1)}, u32[]{:S(2)}, u32[]{:S(2)}) %collective-permute-start.3) | collective-permute-done | bytes 184352 | tf_op jit(solution)/shard_map/ppermute | solution.py:69
  52.6 3.4 %collective-permute-start.4 = (bf16[216,1280]{1,0:T(8,128)(2,1)S(1)}, bf16[216,1280]{1,0:T(8,128)(2,1)S(1)}, u32[]{:S(2)}, u32[]{:S(2)}) collective-permute-start(bf16[216,1280]{1,0:T(8,128)(2,1)S(1)} %pad_maximum_fusion.1), channel_id=1, source_target_pairs={{0,7},{1,0},{2,1},{3,2},{4,3},{5,4},{6,5},{7,6},{8,15},{9,8},{10,9... | collective-permute-start | bytes 1658888 | tf_op jit(solution)/shard_map/ppermute | solution.py:69
  56.1 4.8 %collective-permute-start.5 = (bf16[144,1280]{1,0:T(8,128)(2,1)S(1)}, bf16[144,1280]{1,0:T(8,128)(2,1)S(1)}, u32[]{:S(2)}, u32[]{:S(2)}) collective-permute-start(bf16[144,1280]{1,0:T(8,128)(2,1)S(1)} %pad_maximum_fusion.5), channel_id=1, source_target_pairs={{0,1},{1,2},{2,3},{3,4},{4,5},{5,6},{6,7},{7,0},{8,9},{9,10},{10,1... | collective-permute-start | bytes 1105928 | tf_op jit(solution)/shard_map/ppermute | solution.py:69
  69.2 2.8 %subtract_convert_fusion = bf16[576,768]{1,0:T(8,128)(2,1)S(1)} fusion(bf16[576,1280]{1,0:T(8,128)(2,1)} %constant_dynamic-update-slice_fusion, s32[768]{0:T(1024)S(1)} %add.187, f32[]{:T(128)} %bitcast.7, f32[]{:T(128)} %bitcast, s32[576]{0:T(1024)S(1)} %fusion.16, bf16[384,1152]{1,0:T(8,128)(2,1)S(1)} %collective-permute-done.6, ...), kind=kOutput, calls=%fused_computation.5 | convolution fusion | flops 1026736128 | bytes 3987712 | tf_op jit(solution)/shard_map/dot_general | solution.py:110
  73.0 3.9 %collective-permute-start.7 = (bf16[216,1152]{1,0:T(8,128)(2,1)S(1)}, bf16[216,1152]{1,0:T(8,128)(2,1)S(1)}, u32[]{:S(2)}, u32[]{:S(2)}) collective-permute-start(bf16[216,1152]{1,0:T(8,128)(2,1)S(1)} %slice.74), channel_id=1, source_target_pairs={{0,1},{1,2},{2,3},{3,4},{4,5},{5,6},{6,7},{7,0},{8,9},{9,10},{10,1... | collective-permute-start | bytes 1493000 | tf_op jit(solution)/shard_map/ppermute | solution.py:69
  77.0 2.3 %convolution_convert_fusion = bf16[384,1152]{1,0:T(8,128)(2,1)S(1)} fusion(bf16[576,1280]{1,0:T(8,128)(2,1)} %constant_dynamic-update-slice_fusion, bf16[576,768]{1,0:T(8,128)(2,1)S(1)} %subtract_convert_fusion), kind=kOutput, calls=%fused_computation.2 | convolution fusion | flops 510050304 | bytes 2654208 | tf_op jit(solution)/shard_map/dot_general | solution.py:115
  81.2 3.1 %collective-permute-start.8 = (bf16[144,1152]{1,0:T(8,128)(2,1)S(1)}, bf16[144,1152]{1,0:T(8,128)(2,1)S(1)}, u32[]{:S(2)}, u32[]{:S(2)}) collective-permute-start(bf16[144,1152]{1,0:T(8,128)(2,1)S(1)} %slice.76), channel_id=1, source_target_pairs={{0,7},{1,0},{2,1},{3,2},{4,3},{5,4},{6,5},{7,6},{8,15},{9,8},{10,9... | collective-permute-start | bytes 995336 | tf_op jit(solution)/shard_map/ppermute | solution.py:69
  85.0 8.3 %collective-permute-done.8 = bf16[144,1152]{1,0:T(8,128)(2,1)S(1)} collective-permute-done((bf16[144,1152]{1,0:T(8,128)(2,1)S(1)}, bf16[144,1152]{1,0:T(8,128)(2,1)S(1)}, u32[]{:S(2)}, u32[]{:S(2)}) %collective-permute-start.8) | collective-permute-done | bytes 331808 | tf_op jit(solution)/shard_map/ppermute | solution.py:69
  94.1 6.5 %collective-permute-start.10 = (bf16[72,1152]{1,0:T(8,128)(2,1)S(1)}, bf16[72,1152]{1,0:T(8,128)(2,1)S(1)}, u32[]{:S(2)}, u32[]{:S(2)}) collective-permute-start(bf16[72,1152]{1,0:T(8,128)(2,1)S(1)} %get-tuple-element.21), channel_id=1, source_target_pairs={{0,3},{1,4},{2,5},{3,6},{4,7},{5,0},{6,1},{7,2},{8,11},{9,12},{10,... | collective-permute-start | bytes 497672 | tf_op jit(solution)/shard_map/ppermute | solution.py:69
  100.6 2.3 %collective-permute-start.9 = (bf16[72,1152]{1,0:T(8,128)(2,1)S(1)}, bf16[72,1152]{1,0:T(8,128)(2,1)S(1)}, u32[]{:S(2)}, u32[]{:S(2)}) collective-permute-start(bf16[72,1152]{1,0:T(8,128)(2,1)S(1)} %get-tuple-element.20), channel_id=1, source_target_pairs={{0,5},{1,6},{2,7},{3,0},{4,1},{5,2},{6,3},{7,4},{8,13},{9,14},{10,... | collective-permute-start | bytes 497672 | tf_op jit(solution)/shard_map/ppermute | solution.py:69
  103.0 3.2 %fusion = bf16[384,1152]{1,0:T(8,128)(2,1)} fusion(bf16[384,1152]{1,0:T(8,128)(2,1)S(1)} %collective-permute-done.13, bf16[576,1280]{1,0:T(8,128)(2,1)} %constant_dynamic-update-slice_fusion, bf16[576,768]{1,0:T(8,128)(2,1)S(1)} %subtract_convert_fusion), kind=kOutput, calls=%fused_computation.1 | convolution fusion | flops 510935040 | bytes 3538944 | tf_op jit(solution)/shard_map/dot_general | solution.py:115
  106.2 4.9 %all-to-all-start.2 = ((bf16[4,96,1152]{2,1,0:T(8,128)(2,1)}), bf16[4,96,1152]{2,1,0:T(8,128)(2,1)S(1)}, u32[]{:S(2)}, u32[]{:S(2)}) async-start(bf16[4,96,1152]{2,1,0:T(8,128)(2,1)} %bitcast.5), calls=%async_computation.2 | async-start | bytes 1769472 | tf_op jit(solution)/shard_map/all_to_all | solution.py:48
  111.1 6.0 %collective-permute-done.9 = bf16[72,1152]{1,0:T(8,128)(2,1)S(1)} collective-permute-done((bf16[72,1152]{1,0:T(8,128)(2,1)S(1)}, bf16[72,1152]{1,0:T(8,128)(2,1)S(1)}, u32[]{:S(2)}, u32[]{:S(2)}) %collective-permute-start.9) | collective-permute-done | bytes 165920 | tf_op jit(solution)/shard_map/ppermute | solution.py:69
  118.1 3.4 %collective-permute-start.12 = (bf16[24,1152]{1,0:T(8,128)(2,1)S(1)}, bf16[24,1152]{1,0:T(8,128)(2,1)S(1)}, u32[]{:S(2)}, u32[]{:S(2)}) collective-permute-start(bf16[24,1152]{1,0:T(8,128)(2,1)S(1)} %get-tuple-element.23), channel_id=1, source_target_pairs={{0,400},{8,576},{16,584},{192,592},{200,0},{208,8},{384,16},{392,1... | collective-permute-start | bytes 165896 | tf_op jit(solution)/shard_map/ppermute | solution.py:69
  121.5 6.4 %collective-permute-start.11 = (bf16[24,1152]{1,0:T(8,128)(2,1)S(1)}, bf16[24,1152]{1,0:T(8,128)(2,1)S(1)}, u32[]{:S(2)}, u32[]{:S(2)}) collective-permute-start(bf16[24,1152]{1,0:T(8,128)(2,1)S(1)} %get-tuple-element.22), channel_id=1, source_target_pairs={{0,200},{8,208},{16,384},{192,392},{200,400},{208,576},{384,584},{... | collective-permute-start | bytes 165896 | tf_op jit(solution)/shard_map/ppermute | solution.py:69
  129.0 4.1 %all-to-all-start.3 = ((bf16[4,24,1152]{2,1,0:T(8,128)(2,1)}), bf16[4,24,1152]{2,1,0:T(8,128)(2,1)S(1)}, u32[]{:S(2)}, u32[]{:S(2)}) async-start(bf16[4,24,1152]{2,1,0:T(8,128)(2,1)} %bitcast.6), calls=%async_computation.3 | async-start | bytes 442368 | tf_op jit(solution)/shard_map/all_to_all | solution.py:48
  134.0 6.6 %all-to-all-done.3 = bf16[4,24,1152]{2,1,0:T(8,128)(2,1)S(1)} async-done(((bf16[4,24,1152]{2,1,0:T(8,128)(2,1)}), bf16[4,24,1152]{2,1,0:T(8,128)(2,1)S(1)}, u32[]{:S(2)}, u32[]{:S(2)}) %all-to-all-start.3) | async-done | bytes 221216 | tf_op jit(solution)/shard_map/all_to_all | solution.py:48
  (55 shorter events, 22.1 us)
Async XLA Ops:
  2.3 30.5 %all-to-all-start = ((bf16[4,24,1152]{2,1,0:T(8,128)(2,1)}), bf16[4,24,1152]{2,1,0:T(8,128)(2,1)S(1)}, u32[]{:S(2)}, u32[]{:S(2)}) async-start(bf16[4,24,1152]{2,1,0:T(8,128)(2,1)} %get-tuple-element.11), calls=%async_computation | async-start | bytes 442368 | tf_op jit(solution)/shard_map/all_to_all | solution.py:48
  9.5 15.5 %collective-permute-start.1 = (bf16[24,1280]{1,0:T(8,128)(2,1)}, bf16[24,1280]{1,0:T(8,128)(2,1)S(1)}, u32[]{:S(2)}, u32[]{:S(2)}) collective-permute-start(bf16[24,1280]{1,0:T(8,128)(2,1)} %get-tuple-element.10), channel_id=1, source_target_pairs={{0,200},{8,208},{16,384},{192,392},{200,400},{208,576},{384,584},{... | collective-permute-start | bytes 184328 | tf_op jit(solution)/shard_map/ppermute | solution.py:69
  20.2 11.8 %collective-permute-start = (bf16[24,1280]{1,0:T(8,128)(2,1)}, bf16[24,1280]{1,0:T(8,128)(2,1)S(1)}, u32[]{:S(2)}, u32[]{:S(2)}) collective-permute-start(bf16[24,1280]{1,0:T(8,128)(2,1)} %get-tuple-element.10), channel_id=1, source_target_pairs={{0,400},{8,576},{16,584},{192,592},{200,0},{208,8},{384,16},{392,1... | collective-permute-start | bytes 184328 | tf_op jit(solution)/shard_map/ppermute | solution.py:69
  32.8 16.1 %collective-permute-start.2 = (bf16[72,1280]{1,0:T(8,128)(2,1)S(1)}, bf16[72,1280]{1,0:T(8,128)(2,1)S(1)}, u32[]{:S(2)}, u32[]{:S(2)}) collective-permute-start(bf16[72,1280]{1,0:T(8,128)(2,1)S(1)} %pad_maximum_fusion.6), channel_id=1, source_target_pairs={{0,3},{1,4},{2,5},{3,6},{4,7},{5,0},{6,1},{7,2},{8,11},{9,12},{10,... | collective-permute-start | bytes 552968 | tf_op jit(solution)/shard_map/ppermute | solution.py:69
  38.3 14.3 %collective-permute-start.3 = (bf16[72,1280]{1,0:T(8,128)(2,1)S(1)}, bf16[72,1280]{1,0:T(8,128)(2,1)S(1)}, u32[]{:S(2)}, u32[]{:S(2)}) collective-permute-start(bf16[72,1280]{1,0:T(8,128)(2,1)S(1)} %pad_maximum_fusion.6), channel_id=1, source_target_pairs={{0,5},{1,6},{2,7},{3,0},{4,1},{5,2},{6,3},{7,4},{8,13},{9,14},{10,... | collective-permute-start | bytes 552968 | tf_op jit(solution)/shard_map/ppermute | solution.py:69
  44.1 18.1 %all-to-all-start.1 = ((bf16[4,96,1152]{2,1,0:T(8,128)(2,1)}), bf16[4,96,1152]{2,1,0:T(8,128)(2,1)S(1)}, u32[]{:S(2)}, u32[]{:S(2)}) async-start(bf16[4,96,1152]{2,1,0:T(8,128)(2,1)} %broadcast_in_dim.2), calls=%async_computation.1 | async-start | bytes 1769472 | tf_op jit(solution)/shard_map/all_to_all | solution.py:48
  52.6 13.7 %collective-permute-start.4 = (bf16[216,1280]{1,0:T(8,128)(2,1)S(1)}, bf16[216,1280]{1,0:T(8,128)(2,1)S(1)}, u32[]{:S(2)}, u32[]{:S(2)}) collective-permute-start(bf16[216,1280]{1,0:T(8,128)(2,1)S(1)} %pad_maximum_fusion.1), channel_id=1, source_target_pairs={{0,7},{1,0},{2,1},{3,2},{4,3},{5,4},{6,5},{7,6},{8,15},{9,8},{10,9... | collective-permute-start | bytes 1658888 | tf_op jit(solution)/shard_map/ppermute | solution.py:69
  56.1 11.1 %collective-permute-start.5 = (bf16[144,1280]{1,0:T(8,128)(2,1)S(1)}, bf16[144,1280]{1,0:T(8,128)(2,1)S(1)}, u32[]{:S(2)}, u32[]{:S(2)}) collective-permute-start(bf16[144,1280]{1,0:T(8,128)(2,1)S(1)} %pad_maximum_fusion.5), channel_id=1, source_target_pairs={{0,1},{1,2},{2,3},{3,4},{4,5},{5,6},{6,7},{7,0},{8,9},{9,10},{10,1... | collective-permute-start | bytes 1105928 | tf_op jit(solution)/shard_map/ppermute | solution.py:69
  62.2 7.0 %collective-permute-start.6 = (bf16[384,1152]{1,0:T(8,128)(2,1)S(1)}, bf16[384,1152]{1,0:T(8,128)(2,1)S(1)}, u32[]{:S(2)}, u32[]{:S(2)}) collective-permute-start(bf16[384,1152]{1,0:T(8,128)(2,1)S(1)} %bitcast.8), channel_id=1, source_target_pairs={{0,24},{24,0},{1,25},{25,1},{2,26},{26,2},{3,27},{27,3},{4,28},{28... | collective-permute-start | bytes 2654216 | tf_op jit(solution)/shard_map/ppermute | solution.py:69
  73.0 20.3 %collective-permute-start.7 = (bf16[216,1152]{1,0:T(8,128)(2,1)S(1)}, bf16[216,1152]{1,0:T(8,128)(2,1)S(1)}, u32[]{:S(2)}, u32[]{:S(2)}) collective-permute-start(bf16[216,1152]{1,0:T(8,128)(2,1)S(1)} %slice.74), channel_id=1, source_target_pairs={{0,1},{1,2},{2,3},{3,4},{4,5},{5,6},{6,7},{7,0},{8,9},{9,10},{10,1... | collective-permute-start | bytes 1493000 | tf_op jit(solution)/shard_map/ppermute | solution.py:69
  79.2 23.8 %collective-permute-start.13 = (bf16[384,1152]{1,0:T(8,128)(2,1)S(1)}, bf16[384,1152]{1,0:T(8,128)(2,1)S(1)}, u32[]{:S(2)}, u32[]{:S(2)}) collective-permute-start(bf16[384,1152]{1,0:T(8,128)(2,1)S(1)} %convolution_convert_fusion), channel_id=1, source_target_pairs={{0,24},{24,0},{1,25},{25,1},{2,26},{26,2},{3,27},{27,3},{4,28},{28... | collective-permute-start | bytes 2654216 | tf_op jit(solution)/shard_map/ppermute | solution.py:69
  81.2 12.1 %collective-permute-start.8 = (bf16[144,1152]{1,0:T(8,128)(2,1)S(1)}, bf16[144,1152]{1,0:T(8,128)(2,1)S(1)}, u32[]{:S(2)}, u32[]{:S(2)}) collective-permute-start(bf16[144,1152]{1,0:T(8,128)(2,1)S(1)} %slice.76), channel_id=1, source_target_pairs={{0,7},{1,0},{2,1},{3,2},{4,3},{5,4},{6,5},{7,6},{8,15},{9,8},{10,9... | collective-permute-start | bytes 995336 | tf_op jit(solution)/shard_map/ppermute | solution.py:69
  93.3 0.7 copy-start.2
  94.1 17.0 %collective-permute-start.10 = (bf16[72,1152]{1,0:T(8,128)(2,1)S(1)}, bf16[72,1152]{1,0:T(8,128)(2,1)S(1)}, u32[]{:S(2)}, u32[]{:S(2)}) collective-permute-start(bf16[72,1152]{1,0:T(8,128)(2,1)S(1)} %get-tuple-element.21), channel_id=1, source_target_pairs={{0,3},{1,4},{2,5},{3,6},{4,7},{5,0},{6,1},{7,2},{8,11},{9,12},{10,... | collective-permute-start | bytes 497672 | tf_op jit(solution)/shard_map/ppermute | solution.py:69
  100.6 16.4 %collective-permute-start.9 = (bf16[72,1152]{1,0:T(8,128)(2,1)S(1)}, bf16[72,1152]{1,0:T(8,128)(2,1)S(1)}, u32[]{:S(2)}, u32[]{:S(2)}) collective-permute-start(bf16[72,1152]{1,0:T(8,128)(2,1)S(1)} %get-tuple-element.20), channel_id=1, source_target_pairs={{0,5},{1,6},{2,7},{3,0},{4,1},{5,2},{6,3},{7,4},{8,13},{9,14},{10,... | collective-permute-start | bytes 497672 | tf_op jit(solution)/shard_map/ppermute | solution.py:69
  106.2 21.7 %copy-start.4 = (f32[24,1]{1,0:T(8,128)S(1)}, f32[24,1]{1,0:T(8,128)}, u32[]{:S(2)}) copy-start(f32[24,1]{1,0:T(8,128)} %get-tuple-element.16) | copy-start | bytes 292
  106.2 21.9 %copy-start.3 = (f32[24,1]{1,0:T(8,128)S(1)}, f32[24,1]{1,0:T(8,128)}, u32[]{:S(2)}) copy-start(f32[24,1]{1,0:T(8,128)} %get-tuple-element.17) | copy-start | bytes 292
  106.2 22.0 %all-to-all-start.2 = ((bf16[4,96,1152]{2,1,0:T(8,128)(2,1)}), bf16[4,96,1152]{2,1,0:T(8,128)(2,1)S(1)}, u32[]{:S(2)}, u32[]{:S(2)}) async-start(bf16[4,96,1152]{2,1,0:T(8,128)(2,1)} %bitcast.5), calls=%async_computation.2 | async-start | bytes 1769472 | tf_op jit(solution)/shard_map/all_to_all | solution.py:48
  111.1 22.0 %copy-start = (bf16[24,1152]{1,0:T(8,128)(2,1)S(1)}, bf16[24,1152]{1,0:T(8,128)(2,1)}, u32[]{:S(2)}) copy-start(bf16[24,1152]{1,0:T(8,128)(2,1)} %img_ref.1) | copy-start | bytes 165892
  118.1 22.6 %copy-start.1 = (bf16[24,1152]{1,0:T(8,128)(2,1)S(1)}, bf16[24,1152]{1,0:T(8,128)(2,1)}, u32[]{:S(2)}) copy-start(bf16[24,1152]{1,0:T(8,128)(2,1)} %txt_ref.1) | copy-start | bytes 165892
  118.1 15.0 %collective-permute-start.12 = (bf16[24,1152]{1,0:T(8,128)(2,1)S(1)}, bf16[24,1152]{1,0:T(8,128)(2,1)S(1)}, u32[]{:S(2)}, u32[]{:S(2)}) collective-permute-start(bf16[24,1152]{1,0:T(8,128)(2,1)S(1)} %get-tuple-element.23), channel_id=1, source_target_pairs={{0,400},{8,576},{16,584},{192,592},{200,0},{208,8},{384,16},{392,1... | collective-permute-start | bytes 165896 | tf_op jit(solution)/shard_map/ppermute | solution.py:69
  121.5 11.6 %collective-permute-start.11 = (bf16[24,1152]{1,0:T(8,128)(2,1)S(1)}, bf16[24,1152]{1,0:T(8,128)(2,1)S(1)}, u32[]{:S(2)}, u32[]{:S(2)}) collective-permute-start(bf16[24,1152]{1,0:T(8,128)(2,1)S(1)} %get-tuple-element.22), channel_id=1, source_target_pairs={{0,200},{8,208},{16,384},{192,392},{200,400},{208,576},{384,584},{... | collective-permute-start | bytes 165896 | tf_op jit(solution)/shard_map/ppermute | solution.py:69
  129.0 11.6 %all-to-all-start.3 = ((bf16[4,24,1152]{2,1,0:T(8,128)(2,1)}), bf16[4,24,1152]{2,1,0:T(8,128)(2,1)S(1)}, u32[]{:S(2)}, u32[]{:S(2)}) async-start(bf16[4,24,1152]{2,1,0:T(8,128)(2,1)} %bitcast.6), calls=%async_computation.3 | async-start | bytes 442368 | tf_op jit(solution)/shard_map/all_to_all | solution.py:48

commit v4 on v3

--- a/solution.py
+++ b/solution.py
@@ -39,6 +39,37 @@
 def project_back(raw, inverse, dnorm):
     hat = raw.astype(F32) * inverse
     return (dnorm - hat * jnp.sum(hat * dnorm, axis=-1, keepdims=True)) * inverse
+
+
+def pair_products(
+    packed_ref, txt_ref, column_ref, scalar_ref,
+    mine_ref, before_ref, after_ref, own_part_ref, far_part_ref, grad,
+):
+    width = txt_ref.shape[1]
+    half = own_part_ref.shape[0]
+    y = mine_ref.shape[1]
+    step = packed_ref.shape[0] // 2
+    for start in (0, step):
+        rows = slice(start, start + step)
+        scores = lax.dot_general(
+            packed_ref[rows, :width], txt_ref[...], (((1,), (1,)), ((), ())), preferred_element_type=F32
+        )
+        mark = packed_ref[rows, width:].astype(F32)
+        positive = (mark[:, 0:1] * 256.0 + mark[:, 1:2] == column_ref[...]).astype(F32)
+        logits = scalar_ref[0] * scores + scalar_ref[1]
+        grad[rows, :] = (jax.nn.sigmoid(logits) - positive).astype(BF)
+    part = jnp.dot(grad[...], txt_ref[...], preferred_element_type=F32)
+    for i in range(3):
+        mine_ref[i] = part[i * y : (i + 1) * y]
+    before_ref[...] = part[3 * y : 6 * y].astype(BF)
+    after_ref[...] = part[6 * y :].astype(BF)
+    for columns, part_ref in ((slice(half, 2 * half), far_part_ref), (slice(0, half), own_part_ref)):
+        part_ref[...] = lax.dot_general(
+            grad[:, columns],
+            packed_ref[:, :width],
+            (((0,), (0,)), ((), ())),
+            preferred_element_type=F32,
+        ).astype(part_ref.dtype)
 
 
 def exchange(blocks, axes):
@@ -94,11 +125,8 @@
     packed = jnp.concatenate([wide, send(wide, "y", -1), send(wide[y:], "y", 1)])
     txt = spread(txt, "x", n_x)
     half = txt.shape[0]
+    packed, txt = lax.optimization_barrier((packed, txt))
     txt = jnp.concatenate([txt, send(txt, "c", 1)])
-
-    img = packed[:, :width]
-    marks = packed[:, width : width + 2].astype(F32)
-    target = (marks[:, :1] * 256.0 + marks[:, 1:]).astype(jnp.int32)
 
     owner = jnp.arange(n_c * n_x * RUN, dtype=jnp.int32)
     at_z = lax.axis_index(Z) // RUN * RUN + owner % RUN
@@ -107,26 +135,28 @@
     col = at_z % n_zl * n_y + lax.axis_index("y")
     block = ((col * (n_z // n_zl) + at_z // n_zl) * n_x + at_x) * n_c + at_c
     columns = block[:, None] * blk + jnp.arange(blk, dtype=jnp.int32)[None, :]
-    scores = lax.dot_general(img, txt, (((1,), (1,)), ((), ())), preferred_element_type=F32)
-    positive = (target == columns.reshape(1, -1)).astype(F32)
-    grad = (jax.nn.sigmoid(temperature * scores + shift) - positive).astype(BF)
-
-    def txt_part(part):
-        return lax.dot_general(part, img, (((0,), (0,)), ((), ())), preferred_element_type=F32)
-
-    away = jnp.dot(grad[3 * y :], txt, preferred_element_type=F32).astype(BF)
-    away, grad = lax.optimization_barrier((away, grad))
-    before, after = send(away[: 3 * y], "y", 1), send(away[3 * y :], "y", -1)
-
-    arrived = send(txt_part(grad[:, half:]), "c", 1)
-    txt_sum = txt_part(grad[:, :half]) + arrived.astype(F32)
+    mine, away, back, own_part, far_part = pl.pallas_call(
+        pair_products,
+        out_shape=[
+            jax.ShapeDtypeStruct((3, y, width), F32),
+            jax.ShapeDtypeStruct((3 * y, width), BF),
+            jax.ShapeDtypeStruct((2 * y, width), BF),
+            jax.ShapeDtypeStruct((half, width), F32),
+            jax.ShapeDtypeStruct((half, width), BF),
+        ],
+        in_specs=[vmem] * 3 + [pl.BlockSpec(memory_space=pltpu.SMEM)],
+        out_specs=[vmem] * 5,
+        scratch_shapes=[pltpu.VMEM((packed.shape[0], 2 * half), BF)],
+        compiler_params=pltpu.CompilerParams(vmem_limit_bytes=24 * 1024 * 1024),
+    )(packed, txt, columns.reshape(1, -1).astype(F32), jnp.stack([temperature, shift]))
+    before, after = send(away, "y", 1), send(back, "y", -1)
+    txt_sum = own_part + send(far_part, "c", 1).astype(F32)
     txt_sum = jnp.sum(scattered(txt_sum, "x", n_x).astype(F32), axis=0)
     txt_sum = jnp.sum(scattered(txt_sum, Z, RUN).astype(F32), axis=0)
 
-    mine = jnp.dot(grad[: 3 * y], txt, preferred_element_type=F32)
-    low = mine[:y] + before[:y].astype(F32)
-    mid = mine[y : 2 * y] + before[y : 2 * y].astype(F32) + after[:y].astype(F32)
-    top = mine[2 * y :] + before[2 * y :].astype(F32) + after[y:].astype(F32)
+    low = mine[0] + before[:y].astype(F32)
+    mid = mine[1] + before[y : 2 * y].astype(F32) + after[:y].astype(F32)
+    top = mine[2] + before[2 * y :].astype(F32) + after[y:].astype(F32)
     mid = mid + send(low, "y", -3).astype(F32) + send(top, "y", 3).astype(F32)
     one, two = send(mid[blk : 2 * blk], Z, RUN), send(mid[2 * blk :], Z, -RUN)
     img_sum = mid[:blk] + one.astype(F32) + two.astype(F32)

time: 143 us -> 144 us (level)
  waiting for transfers between devices: 34.7 us -> 46.9 us
  matrix products: 9.8 us -> 0 us
  Pallas kernels: 1.66 us -> 6.2 us
  local copies, waits for them, and re-layouts: 5.55 us -> 1.21 us
  starting transfers between devices: 81.3 us -> 79 us
    ppermute x14, waiting for transfers between devices: 28.1 us -> 41.3 us  [send(): lax.ppermute(x.astype(BF), axis, [(i, (i + hop) % size) for i in range(si...]
    dot_general x5 -> x0, matrix products: 9.8 us -> none  [the longest x2 5.42 us: txt_part(): lax.dot_general(part, img, (((0,), (0,)), ((), ())), preferred_element_ty...]
    pallas_call x0 -> x1, Pallas kernels: none -> 4.54 us  [on_device(): pl.pallas_call(pair_products, out_shape=[jax.ShapeDtypeStruct((3, y, widt...]
    unnamed x14 -> x12, local copies, waits for them, and re-layouts: 3.64 us -> 0.1 us
    ppermute x14, starting transfers between devices: 60.3 us -> 56.9 us  [send(): lax.ppermute(x.astype(BF), axis, [(i, (i + hop) % size) for i in range(si...]
  transfers between devices with their start and end apart: 18 -> 18, of which waited for: 7 -> 11; matrix products, arithmetic and copies ran while one was open for 11% -> 5% of each run, Pallas kernels for 0% -> 0%
where the time goes in v4:
time: 144 us; the launch traced here: 142 us
  starting transfers between devices  79 us (55%)
  waiting for transfers between devices  46.9 us (33%)
  other arithmetic  6.4 us (4%)
  Pallas kernels  6.2 us (4%)
  between operations  2.26 us (2%)
    ppermute x14, starting transfers between devices, send(): lax.ppermute(x.astype(BF), axis, [(i, (i + hop) % size) for i in range(si...  56.9 us
    ppermute x14, waiting for transfers between devices, send(): lax.ppermute(x.astype(BF), axis, [(i, (i + hop) % size) for i in range(si...  41.3 us
    all_to_all x4, starting transfers between devices, exchange(): lax.all_to_all(blocks, axes, split_axis=0, concat_axis=0, axis_index_grou...  22.1 us
    all_to_all x4, waiting for transfers between devices, exchange(): lax.all_to_all(blocks, axes, split_axis=0, concat_axis=0, axis_index_grou...  5.58 us
    pallas_call x1, Pallas kernels, on_device(): pl.pallas_call(pair_products, out_shape=[jax.ShapeDtypeStruct((3, y, widt...  4.54 us
  transfers between devices with their start and end apart: 18, of which 11 were waited for; matrix products, arithmetic and copies ran while one was open for 5% of the time, Pallas kernels for 0%

profile of v4, /device:TPU:6, one launch (start us, length us, event | category | flops | bytes accessed | tf_op | source)
XLA Modules:
  0.0 142.0 jit_solution(16922642941102017038)
XLA Ops:
  2.3 7.3 %all-to-all-start = ((bf16[4,24,1152]{2,1,0:T(8,128)(2,1)}), bf16[4,24,1152]{2,1,0:T(8,128)(2,1)S(1)}, u32[]{:S(2)}, u32[]{:S(2)}) async-start(bf16[4,24,1152]{2,1,0:T(8,128)(2,1)} %get-tuple-element.16), calls=%async_computation | async-start | bytes 442368 | tf_op jit(solution)/shard_map/all_to_all | solution.py:79
  9.5 10.6 %collective-permute-start.1 = (bf16[24,1280]{1,0:T(8,128)(2,1)}, bf16[24,1280]{1,0:T(8,128)(2,1)S(1)}, u32[]{:S(2)}, u32[]{:S(2)}) collective-permute-start(bf16[24,1280]{1,0:T(8,128)(2,1)} %get-tuple-element.15), channel_id=1, source_target_pairs={{0,200},{8,208},{16,384},{192,392},{200,400},{208,576},{384,584},{... | collective-permute-start | bytes 184328 | tf_op jit(solution)/shard_map/ppermute | solution.py:100
  20.2 3.2 %collective-permute-start = (bf16[24,1280]{1,0:T(8,128)(2,1)}, bf16[24,1280]{1,0:T(8,128)(2,1)S(1)}, u32[]{:S(2)}, u32[]{:S(2)}) collective-permute-start(bf16[24,1280]{1,0:T(8,128)(2,1)} %get-tuple-element.15), channel_id=1, source_target_pairs={{0,400},{8,576},{16,584},{192,592},{200,0},{208,8},{384,16},{392,1... | collective-permute-start | bytes 184328 | tf_op jit(solution)/shard_map/ppermute | solution.py:100
  25.1 6.8 %collective-permute-done = bf16[24,1280]{1,0:T(8,128)(2,1)S(1)} collective-permute-done((bf16[24,1280]{1,0:T(8,128)(2,1)}, bf16[24,1280]{1,0:T(8,128)(2,1)S(1)}, u32[]{:S(2)}, u32[]{:S(2)}) %collective-permute-start) | collective-permute-done | bytes 61472 | tf_op jit(solution)/shard_map/ppermute | solution.py:100
  32.8 6.9 %collective-permute-start.3 = (bf16[72,1280]{1,0:T(8,128)(2,1)S(1)}, bf16[72,1280]{1,0:T(8,128)(2,1)S(1)}, u32[]{:S(2)}, u32[]{:S(2)}) collective-permute-start(bf16[72,1280]{1,0:T(8,128)(2,1)S(1)} %pad_maximum_fusion.3), channel_id=1, source_target_pairs={{0,5},{1,6},{2,7},{3,0},{4,1},{5,2},{6,3},{7,4},{8,13},{9,14},{10,... | collective-permute-start | bytes 552968 | tf_op jit(solution)/shard_map/ppermute | solution.py:100
  39.7 1.9 %collective-permute-start.2 = (bf16[72,1280]{1,0:T(8,128)(2,1)S(1)}, bf16[72,1280]{1,0:T(8,128)(2,1)S(1)}, u32[]{:S(2)}, u32[]{:S(2)}) collective-permute-start(bf16[72,1280]{1,0:T(8,128)(2,1)S(1)} %pad_maximum_fusion.3), channel_id=1, source_target_pairs={{0,3},{1,4},{2,5},{3,6},{4,7},{5,0},{6,1},{7,2},{8,11},{9,12},{10,... | collective-permute-start | bytes 552968 | tf_op jit(solution)/shard_map/ppermute | solution.py:100
  42.7 4.8 %all-to-all-start.1 = ((bf16[4,96,1152]{2,1,0:T(8,128)(2,1)}), bf16[4,96,1152]{2,1,0:T(8,128)(2,1)S(1)}, u32[]{:S(2)}, u32[]{:S(2)}) async-start(bf16[4,96,1152]{2,1,0:T(8,128)(2,1)} %broadcast_in_dim.2), calls=%async_computation.1 | async-start | bytes 1769472 | tf_op jit(solution)/shard_map/all_to_all | solution.py:79
  48.4 4.0 %collective-permute-start.5 = (bf16[144,1280]{1,0:T(8,128)(2,1)S(1)}, bf16[144,1280]{1,0:T(8,128)(2,1)S(1)}, u32[]{:S(2)}, u32[]{:S(2)}) collective-permute-start(bf16[144,1280]{1,0:T(8,128)(2,1)S(1)} %pad_maximum_fusion.2), channel_id=1, source_target_pairs={{0,1},{1,2},{2,3},{3,4},{4,5},{5,6},{6,7},{7,0},{8,9},{9,10},{10,1... | collective-permute-start | bytes 1105928 | tf_op jit(solution)/shard_map/ppermute | solution.py:100
  52.4 2.3 %collective-permute-done.2 = bf16[72,1280]{1,0:T(8,128)(2,1)S(1)} collective-permute-done((bf16[72,1280]{1,0:T(8,128)(2,1)S(1)}, bf16[72,1280]{1,0:T(8,128)(2,1)S(1)}, u32[]{:S(2)}, u32[]{:S(2)}) %collective-permute-start.2) | collective-permute-done | bytes 184352 | tf_op jit(solution)/shard_map/ppermute | solution.py:100
  54.8 1.9 %collective-permute-start.4 = (bf16[216,1280]{1,0:T(8,128)(2,1)S(1)}, bf16[216,1280]{1,0:T(8,128)(2,1)S(1)}, u32[]{:S(2)}, u32[]{:S(2)}) collective-permute-start(bf16[216,1280]{1,0:T(8,128)(2,1)S(1)} %pad_maximum_fusion.1), channel_id=1, source_target_pairs={{0,7},{1,0},{2,1},{3,2},{4,3},{5,4},{6,5},{7,6},{8,15},{9,8},{10,9... | collective-permute-start | bytes 1658888 | tf_op jit(solution)/shard_map/ppermute | solution.py:100
  56.8 12.9 %collective-permute-done.4 = bf16[216,1280]{1,0:T(8,128)(2,1)S(1)} collective-permute-done((bf16[216,1280]{1,0:T(8,128)(2,1)S(1)}, bf16[216,1280]{1,0:T(8,128)(2,1)S(1)}, u32[]{:S(2)}, u32[]{:S(2)}) %collective-permute-start.4) | collective-permute-done | bytes 552992 | tf_op jit(solution)/shard_map/ppermute | solution.py:100
  74.3 4.5 %shard_map.69 = (f32[3,72,1152]{2,1,0:T(8,128)S(1)}, bf16[216,1152]{1,0:T(8,128)(2,1)S(1)}, bf16[144,1152]{1,0:T(8,128)(2,1)S(1)}, f32[384,1152]{1,0:T(8,128)S(1)}, bf16[384,1152]{1,0:T(8,128)(2,1)S(1)}) custom-call(bf16[576,1280]{1,0:T(8,128)(2,1)S(1)} %constant_dynamic-update-slice_fusion.packed_ref, bf16[768,1152]{1,0:T(8,128)(2,1)S(1)} %pad_maximum_fusion.txt_ref, ...), custom_call_target="tpu_custom_call" | custom-call | tf_op jit(solution)/shard_map/pallas_call | solution.py:138
  80.7 2.1 %collective-permute-start.13 = (bf16[384,1152]{1,0:T(8,128)(2,1)S(1)}, bf16[384,1152]{1,0:T(8,128)(2,1)S(1)}, u32[]{:S(2)}, u32[]{:S(2)}) collective-permute-start(bf16[384,1152]{1,0:T(8,128)(2,1)S(1)} %get-tuple-element.26), channel_id=1, source_target_pairs={{0,24},{24,0},{1,25},{25,1},{2,26},{26,2},{3,27},{27,3},{4,28},{28... | collective-permute-start | bytes 2654216 | tf_op jit(solution)/shard_map/ppermute | solution.py:100
  82.8 5.0 %collective-permute-start.8 = (bf16[144,1152]{1,0:T(8,128)(2,1)S(1)}, bf16[144,1152]{1,0:T(8,128)(2,1)S(1)}, u32[]{:S(2)}, u32[]{:S(2)}) collective-permute-start(bf16[144,1152]{1,0:T(8,128)(2,1)S(1)} %get-tuple-element.23), channel_id=1, source_target_pairs={{0,7},{1,0},{2,1},{3,2},{4,3},{5,4},{6,5},{7,6},{8,15},{9,8},{10,9... | collective-permute-start | bytes 995336 | tf_op jit(solution)/shard_map/ppermute | solution.py:100
  87.8 7.7 %collective-permute-done.8 = bf16[144,1152]{1,0:T(8,128)(2,1)S(1)} collective-permute-done((bf16[144,1152]{1,0:T(8,128)(2,1)S(1)}, bf16[144,1152]{1,0:T(8,128)(2,1)S(1)}, u32[]{:S(2)}, u32[]{:S(2)}) %collective-permute-start.8) | collective-permute-done | bytes 331808 | tf_op jit(solution)/shard_map/ppermute | solution.py:100
  95.6 3.8 %collective-permute-start.9 = (bf16[72,1152]{1,0:T(8,128)(2,1)S(1)}, bf16[72,1152]{1,0:T(8,128)(2,1)S(1)}, u32[]{:S(2)}, u32[]{:S(2)}) collective-permute-start(bf16[72,1152]{1,0:T(8,128)(2,1)S(1)} %get-tuple-element.30), channel_id=1, source_target_pairs={{0,5},{1,6},{2,7},{3,0},{4,1},{5,2},{6,3},{7,4},{8,13},{9,14},{10,... | collective-permute-start | bytes 497672 | tf_op jit(solution)/shard_map/ppermute | solution.py:100
  99.5 3.8 %collective-permute-start.10 = (bf16[72,1152]{1,0:T(8,128)(2,1)S(1)}, bf16[72,1152]{1,0:T(8,128)(2,1)}, u32[]{:S(2)}, u32[]{:S(2)}) collective-permute-start(bf16[72,1152]{1,0:T(8,128)(2,1)S(1)} %get-tuple-element.31), channel_id=1, source_target_pairs={{0,3},{1,4},{2,5},{3,6},{4,7},{5,0},{6,1},{7,2},{8,11},{9,12},{10,... | collective-permute-start | bytes 497672 | tf_op jit(solution)/shard_map/ppermute | solution.py:100
  104.4 4.9 %all-to-all-start.2 = ((bf16[4,96,1152]{2,1,0:T(8,128)(2,1)}), bf16[4,96,1152]{2,1,0:T(8,128)(2,1)S(1)}, u32[]{:S(2)}, u32[]{:S(2)}) async-start(bf16[4,96,1152]{2,1,0:T(8,128)(2,1)} %bitcast.7), calls=%async_computation.2 | async-start | bytes 1769472 | tf_op jit(solution)/shard_map/all_to_all | solution.py:79
  109.3 2.4 %collective-permute-done.9 = bf16[72,1152]{1,0:T(8,128)(2,1)S(1)} collective-permute-done((bf16[72,1152]{1,0:T(8,128)(2,1)S(1)}, bf16[72,1152]{1,0:T(8,128)(2,1)S(1)}, u32[]{:S(2)}, u32[]{:S(2)}) %collective-permute-start.9) | collective-permute-done | bytes 165920 | tf_op jit(solution)/shard_map/ppermute | solution.py:100
  111.7 4.8 %collective-permute-done.10 = bf16[72,1152]{1,0:T(8,128)(2,1)} collective-permute-done((bf16[72,1152]{1,0:T(8,128)(2,1)S(1)}, bf16[72,1152]{1,0:T(8,128)(2,1)}, u32[]{:S(2)}, u32[]{:S(2)}) %collective-permute-start.10) | collective-permute-done | bytes 165920 | tf_op jit(solution)/shard_map/ppermute | solution.py:100
  117.6 6.2 %collective-permute-start.11 = (bf16[24,1152]{1,0:T(8,128)(2,1)S(1)}, bf16[24,1152]{1,0:T(8,128)(2,1)S(1)}, u32[]{:S(2)}, u32[]{:S(2)}) collective-permute-start(bf16[24,1152]{1,0:T(8,128)(2,1)S(1)} %get-tuple-element.32), channel_id=1, source_target_pairs={{0,200},{8,208},{16,384},{192,392},{200,400},{208,576},{384,584},{... | collective-permute-start | bytes 165896 | tf_op jit(solution)/shard_map/ppermute | solution.py:100
  123.8 3.6 %collective-permute-start.12 = (bf16[24,1152]{1,0:T(8,128)(2,1)S(1)}, bf16[24,1152]{1,0:T(8,128)(2,1)S(1)}, u32[]{:S(2)}, u32[]{:S(2)}) collective-permute-start(bf16[24,1152]{1,0:T(8,128)(2,1)S(1)} %get-tuple-element.33), channel_id=1, source_target_pairs={{0,400},{8,576},{16,584},{192,592},{200,0},{208,8},{384,16},{392,1... | collective-permute-start | bytes 165896 | tf_op jit(solution)/shard_map/ppermute | solution.py:100
  128.5 5.2 %all-to-all-start.3 = ((bf16[4,24,1152]{2,1,0:T(8,128)(2,1)}), bf16[4,24,1152]{2,1,0:T(8,128)(2,1)S(1)}, u32[]{:S(2)}, u32[]{:S(2)}) async-start(bf16[4,24,1152]{2,1,0:T(8,128)(2,1)} %bitcast.8), calls=%async_computation.3 | async-start | bytes 442368 | tf_op jit(solution)/shard_map/all_to_all | solution.py:79
  135.4 5.6 %all-to-all-done.3 = bf16[4,24,1152]{2,1,0:T(8,128)(2,1)S(1)} async-done(((bf16[4,24,1152]{2,1,0:T(8,128)(2,1)}), bf16[4,24,1152]{2,1,0:T(8,128)(2,1)S(1)}, u32[]{:S(2)}, u32[]{:S(2)}) %all-to-all-start.3) | async-done | bytes 221216 | tf_op jit(solution)/shard_map/all_to_all | solution.py:79
  (48 shorter events, 17.4 us)
Async XLA Ops:
  2.3 30.5 %all-to-all-start = ((bf16[4,24,1152]{2,1,0:T(8,128)(2,1)}), bf16[4,24,1152]{2,1,0:T(8,128)(2,1)S(1)}, u32[]{:S(2)}, u32[]{:S(2)}) async-start(bf16[4,24,1152]{2,1,0:T(8,128)(2,1)} %get-tuple-element.16), calls=%async_computation | async-start | bytes 442368 | tf_op jit(solution)/shard_map/all_to_all | solution.py:79
  9.5 15.5 %collective-permute-start.1 = (bf16[24,1280]{1,0:T(8,128)(2,1)}, bf16[24,1280]{1,0:T(8,128)(2,1)S(1)}, u32[]{:S(2)}, u32[]{:S(2)}) collective-permute-start(bf16[24,1280]{1,0:T(8,128)(2,1)} %get-tuple-element.15), channel_id=1, source_target_pairs={{0,200},{8,208},{16,384},{192,392},{200,400},{208,576},{384,584},{... | collective-permute-start | bytes 184328 | tf_op jit(solution)/shard_map/ppermute | solution.py:100
  20.2 11.8 %collective-permute-start = (bf16[24,1280]{1,0:T(8,128)(2,1)}, bf16[24,1280]{1,0:T(8,128)(2,1)S(1)}, u32[]{:S(2)}, u32[]{:S(2)}) collective-permute-start(bf16[24,1280]{1,0:T(8,128)(2,1)} %get-tuple-element.15), channel_id=1, source_target_pairs={{0,400},{8,576},{16,584},{192,592},{200,0},{208,8},{384,16},{392,1... | collective-permute-start | bytes 184328 | tf_op jit(solution)/shard_map/ppermute | solution.py:100
  32.8 15.6 %collective-permute-start.3 = (bf16[72,1280]{1,0:T(8,128)(2,1)S(1)}, bf16[72,1280]{1,0:T(8,128)(2,1)S(1)}, u32[]{:S(2)}, u32[]{:S(2)}) collective-permute-start(bf16[72,1280]{1,0:T(8,128)(2,1)S(1)} %pad_maximum_fusion.3), channel_id=1, source_target_pairs={{0,5},{1,6},{2,7},{3,0},{4,1},{5,2},{6,3},{7,4},{8,13},{9,14},{10,... | collective-permute-start | bytes 552968 | tf_op jit(solution)/shard_map/ppermute | solution.py:100
  39.7 15.0 %collective-permute-start.2 = (bf16[72,1280]{1,0:T(8,128)(2,1)S(1)}, bf16[72,1280]{1,0:T(8,128)(2,1)S(1)}, u32[]{:S(2)}, u32[]{:S(2)}) collective-permute-start(bf16[72,1280]{1,0:T(8,128)(2,1)S(1)} %pad_maximum_fusion.3), channel_id=1, source_target_pairs={{0,3},{1,4},{2,5},{3,6},{4,7},{5,0},{6,1},{7,2},{8,11},{9,12},{10,... | collective-permute-start | bytes 552968 | tf_op jit(solution)/shard_map/ppermute | solution.py:100
  42.7 27.1 %all-to-all-start.1 = ((bf16[4,96,1152]{2,1,0:T(8,128)(2,1)}), bf16[4,96,1152]{2,1,0:T(8,128)(2,1)S(1)}, u32[]{:S(2)}, u32[]{:S(2)}) async-start(bf16[4,96,1152]{2,1,0:T(8,128)(2,1)} %broadcast_in_dim.2), calls=%async_computation.1 | async-start | bytes 1769472 | tf_op jit(solution)/shard_map/all_to_all | solution.py:79
  48.4 21.3 %collective-permute-start.5 = (bf16[144,1280]{1,0:T(8,128)(2,1)S(1)}, bf16[144,1280]{1,0:T(8,128)(2,1)S(1)}, u32[]{:S(2)}, u32[]{:S(2)}) collective-permute-start(bf16[144,1280]{1,0:T(8,128)(2,1)S(1)} %pad_maximum_fusion.2), channel_id=1, source_target_pairs={{0,1},{1,2},{2,3},{3,4},{4,5},{5,6},{6,7},{7,0},{8,9},{9,10},{10,1... | collective-permute-start | bytes 1105928 | tf_op jit(solution)/shard_map/ppermute | solution.py:100
  54.8 14.9 %collective-permute-start.4 = (bf16[216,1280]{1,0:T(8,128)(2,1)S(1)}, bf16[216,1280]{1,0:T(8,128)(2,1)S(1)}, u32[]{:S(2)}, u32[]{:S(2)}) collective-permute-start(bf16[216,1280]{1,0:T(8,128)(2,1)S(1)} %pad_maximum_fusion.1), channel_id=1, source_target_pairs={{0,7},{1,0},{2,1},{3,2},{4,3},{5,4},{6,5},{7,6},{8,15},{9,8},{10,9... | collective-permute-start | bytes 1658888 | tf_op jit(solution)/shard_map/ppermute | solution.py:100
  69.8 4.3 %collective-permute-start.6 = (bf16[384,1152]{1,0:T(8,128)(2,1)S(1)}, bf16[384,1152]{1,0:T(8,128)(2,1)S(1)}, u32[]{:S(2)}, u32[]{:S(2)}) collective-permute-start(bf16[384,1152]{1,0:T(8,128)(2,1)S(1)} %bitcast.25), channel_id=1, source_target_pairs={{0,24},{24,0},{1,25},{25,1},{2,26},{26,2},{3,27},{27,3},{4,28},{28... | collective-permute-start | bytes 2654216 | tf_op jit(solution)/shard_map/ppermute | solution.py:100
  78.8 16.7 %collective-permute-start.7 = (bf16[216,1152]{1,0:T(8,128)(2,1)S(1)}, bf16[216,1152]{1,0:T(8,128)(2,1)S(1)}, u32[]{:S(2)}, u32[]{:S(2)}) collective-permute-start(bf16[216,1152]{1,0:T(8,128)(2,1)S(1)} %get-tuple-element.22), channel_id=1, source_target_pairs={{0,1},{1,2},{2,3},{3,4},{4,5},{5,6},{6,7},{7,0},{8,9},{9,10},{10,1... | collective-permute-start | bytes 1493000 | tf_op jit(solution)/shard_map/ppermute | solution.py:100
  80.7 22.5 %collective-permute-start.13 = (bf16[384,1152]{1,0:T(8,128)(2,1)S(1)}, bf16[384,1152]{1,0:T(8,128)(2,1)S(1)}, u32[]{:S(2)}, u32[]{:S(2)}) collective-permute-start(bf16[384,1152]{1,0:T(8,128)(2,1)S(1)} %get-tuple-element.26), channel_id=1, source_target_pairs={{0,24},{24,0},{1,25},{25,1},{2,26},{26,2},{3,27},{27,3},{4,28},{28... | collective-permute-start | bytes 2654216 | tf_op jit(solution)/shard_map/ppermute | solution.py:100
  82.8 12.7 %collective-permute-start.8 = (bf16[144,1152]{1,0:T(8,128)(2,1)S(1)}, bf16[144,1152]{1,0:T(8,128)(2,1)S(1)}, u32[]{:S(2)}, u32[]{:S(2)}) collective-permute-start(bf16[144,1152]{1,0:T(8,128)(2,1)S(1)} %get-tuple-element.23), channel_id=1, source_target_pairs={{0,7},{1,0},{2,1},{3,2},{4,3},{5,4},{6,5},{7,6},{8,15},{9,8},{10,9... | collective-permute-start | bytes 995336 | tf_op jit(solution)/shard_map/ppermute | solution.py:100
  95.6 16.1 %collective-permute-start.9 = (bf16[72,1152]{1,0:T(8,128)(2,1)S(1)}, bf16[72,1152]{1,0:T(8,128)(2,1)S(1)}, u32[]{:S(2)}, u32[]{:S(2)}) collective-permute-start(bf16[72,1152]{1,0:T(8,128)(2,1)S(1)} %get-tuple-element.30), channel_id=1, source_target_pairs={{0,5},{1,6},{2,7},{3,0},{4,1},{5,2},{6,3},{7,4},{8,13},{9,14},{10,... | collective-permute-start | bytes 497672 | tf_op jit(solution)/shard_map/ppermute | solution.py:100
  99.5 17.1 %collective-permute-start.10 = (bf16[72,1152]{1,0:T(8,128)(2,1)S(1)}, bf16[72,1152]{1,0:T(8,128)(2,1)}, u32[]{:S(2)}, u32[]{:S(2)}) collective-permute-start(bf16[72,1152]{1,0:T(8,128)(2,1)S(1)} %get-tuple-element.31), channel_id=1, source_target_pairs={{0,3},{1,4},{2,5},{3,6},{4,7},{5,0},{6,1},{7,2},{8,11},{9,12},{10,... | collective-permute-start | bytes 497672 | tf_op jit(solution)/shard_map/ppermute | solution.py:100
  104.4 23.0 %copy-start.3 = (f32[24,1]{1,0:T(8,128)S(1)}, f32[24,1]{1,0:T(8,128)}, u32[]{:S(2)}) copy-start(f32[24,1]{1,0:T(8,128)} %get-tuple-element.24) | copy-start | bytes 292
  104.4 23.1 %copy-start.2 = (f32[24,1]{1,0:T(8,128)S(1)}, f32[24,1]{1,0:T(8,128)}, u32[]{:S(2)}) copy-start(f32[24,1]{1,0:T(8,128)} %get-tuple-element.27) | copy-start | bytes 292
  104.4 23.3 %all-to-all-start.2 = ((bf16[4,96,1152]{2,1,0:T(8,128)(2,1)}), bf16[4,96,1152]{2,1,0:T(8,128)(2,1)S(1)}, u32[]{:S(2)}, u32[]{:S(2)}) async-start(bf16[4,96,1152]{2,1,0:T(8,128)(2,1)} %bitcast.7), calls=%async_computation.2 | async-start | bytes 1769472 | tf_op jit(solution)/shard_map/all_to_all | solution.py:79
  109.3 25.2 %copy-start = (bf16[24,1152]{1,0:T(8,128)(2,1)S(1)}, bf16[24,1152]{1,0:T(8,128)(2,1)}, u32[]{:S(2)}) copy-start(bf16[24,1152]{1,0:T(8,128)(2,1)} %img_ref.1) | copy-start | bytes 165892
  117.6 23.5 %copy-start.1 = (bf16[24,1152]{1,0:T(8,128)(2,1)S(1)}, bf16[24,1152]{1,0:T(8,128)(2,1)}, u32[]{:S(2)}) copy-start(bf16[24,1152]{1,0:T(8,128)(2,1)} %txt_ref.1) | copy-start | bytes 165892
  117.6 16.1 %collective-permute-start.11 = (bf16[24,1152]{1,0:T(8,128)(2,1)S(1)}, bf16[24,1152]{1,0:T(8,128)(2,1)S(1)}, u32[]{:S(2)}, u32[]{:S(2)}) collective-permute-start(bf16[24,1152]{1,0:T(8,128)(2,1)S(1)} %get-tuple-element.32), channel_id=1, source_target_pairs={{0,200},{8,208},{16,384},{192,392},{200,400},{208,576},{384,584},{... | collective-permute-start | bytes 165896 | tf_op jit(solution)/shard_map/ppermute | solution.py:100
  123.8 10.7 %collective-permute-start.12 = (bf16[24,1152]{1,0:T(8,128)(2,1)S(1)}, bf16[24,1152]{1,0:T(8,128)(2,1)S(1)}, u32[]{:S(2)}, u32[]{:S(2)}) collective-permute-start(bf16[24,1152]{1,0:T(8,128)(2,1)S(1)} %get-tuple-element.33), channel_id=1, source_target_pairs={{0,400},{8,576},{16,584},{192,592},{200,0},{208,8},{384,16},{392,1... | collective-permute-start | bytes 165896 | tf_op jit(solution)/shard_map/ppermute | solution.py:100
  128.5 12.5 %all-to-all-start.3 = ((bf16[4,24,1152]{2,1,0:T(8,128)(2,1)}), bf16[4,24,1152]{2,1,0:T(8,128)(2,1)S(1)}, u32[]{:S(2)}, u32[]{:S(2)}) async-start(bf16[4,24,1152]{2,1,0:T(8,128)(2,1)} %bitcast.8), calls=%async_computation.3 | async-start | bytes 442368 | tf_op jit(solution)/shard_map/all_to_all | solution.py:79

commit v5 on v3

--- a/solution.py
+++ b/solution.py
@@ -91,7 +91,8 @@
     trio, txt = lax.optimization_barrier((trio, joined(exchange(txt, Z))))
     wide = jnp.concatenate([send(trio, "y", 3), trio, send(trio, "y", -3)])
     y = trio.shape[0]
-    packed = jnp.concatenate([wide, send(wide, "y", -1), send(wide[y:], "y", 1)])
+    part = y // 16 * 8 + 8
+    packed = jnp.concatenate([wide, send(wide[: 2 * y + part], "y", -1), send(wide[part:], "y", 1)])
     txt = spread(txt, "x", n_x)
     half = txt.shape[0]
     txt = jnp.concatenate([txt, send(txt, "c", 1)])
@@ -111,12 +112,12 @@
     positive = (target == columns.reshape(1, -1)).astype(F32)
     grad = (jax.nn.sigmoid(temperature * scores + shift) - positive).astype(BF)
 
-    def txt_part(part):
-        return lax.dot_general(part, img, (((0,), (0,)), ((), ())), preferred_element_type=F32)
+    def txt_part(block):
+        return lax.dot_general(block, img, (((0,), (0,)), ((), ())), preferred_element_type=F32)
 
     away = jnp.dot(grad[3 * y :], txt, preferred_element_type=F32).astype(BF)
     away, grad = lax.optimization_barrier((away, grad))
-    before, after = send(away[: 3 * y], "y", 1), send(away[3 * y :], "y", -1)
+    before, after = send(away[: 2 * y + part], "y", 1), send(away[2 * y + part :], "y", -1)
 
     arrived = send(txt_part(grad[:, half:]), "c", 1)
     txt_sum = txt_part(grad[:, :half]) + arrived.astype(F32)
@@ -124,9 +125,11 @@
     txt_sum = jnp.sum(scattered(txt_sum, Z, RUN).astype(F32), axis=0)
 
     mine = jnp.dot(grad[: 3 * y], txt, preferred_element_type=F32)
-    low = mine[:y] + before[:y].astype(F32)
-    mid = mine[y : 2 * y] + before[y : 2 * y].astype(F32) + after[:y].astype(F32)
-    top = mine[2 * y :] + before[2 * y :].astype(F32) + after[y:].astype(F32)
+    rest = y - part
+    before, after = before.astype(F32), after.astype(F32)
+    low = mine[:y] + before[:y] + jnp.pad(after[:rest], ((part, 0), (0, 0)))
+    mid = mine[y : 2 * y] + before[y : 2 * y] + after[rest : rest + y]
+    top = mine[2 * y :] + jnp.pad(before[2 * y :], ((0, rest), (0, 0))) + after[rest + y :]
     mid = mid + send(low, "y", -3).astype(F32) + send(top, "y", 3).astype(F32)
     one, two = send(mid[blk : 2 * blk], Z, RUN), send(mid[2 * blk :], Z, -RUN)
     img_sum = mid[:blk] + one.astype(F32) + two.astype(F32)

time: 143 us -> 141 us (0.986)
  the two profiles are of different devices: /device:TPU:6 before, /device:TPU:54 now
where the time goes in v5:
time: 141 us; the launch traced here: 140 us
  starting transfers between devices  81.4 us (58%)
  waiting for transfers between devices  28.9 us (20%)
  matrix products  12.4 us (9%)
  other arithmetic  8.62 us (6%)
  local copies, waits for them, and re-layouts  4.93 us (3%)
  between operations  2.3 us (2%)
  Pallas kernels  1.68 us (1%)
    ppermute x14, starting transfers between devices, send(): lax.ppermute(x.astype(BF), axis, [(i, (i + hop) % size) for i in range(si...  58.8 us
    all_to_all x4, starting transfers between devices, exchange(): lax.all_to_all(blocks, axes, split_axis=0, concat_axis=0, axis_index_grou...  22.7 us
    ppermute x14, waiting for transfers between devices, send(): lax.ppermute(x.astype(BF), axis, [(i, (i + hop) % size) for i in range(si...  22.2 us
    all_to_all x4, waiting for transfers between devices, exchange(): lax.all_to_all(blocks, axes, split_axis=0, concat_axis=0, axis_index_grou...  6.68 us
    dot_general x2, matrix products, txt_part(): lax.dot_general(block, img, (((0,), (0,)), ((), ())), preferred_element_t...  5.43 us
    dot_general x1, matrix products, on_device(): lax.dot_general(img, txt, (((1,), (1,)), ((), ())), preferred_element_typ...  3.09 us
  transfers between devices with their start and end apart: 18, of which 8 were waited for; matrix products, arithmetic and copies ran while one was open for 14% of the time, Pallas kernels for 0%

profile of v5, /device:TPU:54, one launch (start us, length us, event | category | flops | bytes accessed | tf_op | source)
XLA Modules:
  0.0 140.2 jit_solution(17014323678770266088)
XLA Ops:
  2.3 7.3 %all-to-all-start = ((bf16[4,24,1152]{2,1,0:T(8,128)(2,1)}), bf16[4,24,1152]{2,1,0:T(8,128)(2,1)S(1)}, u32[]{:S(2)}, u32[]{:S(2)}) async-start(bf16[4,24,1152]{2,1,0:T(8,128)(2,1)} %get-tuple-element.11), calls=%async_computation | async-start | bytes 442368 | tf_op jit(solution)/shard_map/all_to_all | solution.py:48
  9.6 10.6 %collective-permute-start.1 = (bf16[24,1280]{1,0:T(8,128)(2,1)}, bf16[24,1280]{1,0:T(8,128)(2,1)S(1)}, u32[]{:S(2)}, u32[]{:S(2)}) collective-permute-start(bf16[24,1280]{1,0:T(8,128)(2,1)} %get-tuple-element.10), channel_id=1, source_target_pairs={{0,200},{8,208},{16,384},{192,392},{200,400},{208,576},{384,584},{... | collective-permute-start | bytes 184328 | tf_op jit(solution)/shard_map/ppermute | solution.py:69
  20.2 3.2 %collective-permute-start = (bf16[24,1280]{1,0:T(8,128)(2,1)}, bf16[24,1280]{1,0:T(8,128)(2,1)S(1)}, u32[]{:S(2)}, u32[]{:S(2)}) collective-permute-start(bf16[24,1280]{1,0:T(8,128)(2,1)} %get-tuple-element.10), channel_id=1, source_target_pairs={{0,400},{8,576},{16,584},{192,592},{200,0},{208,8},{384,16},{392,1... | collective-permute-start | bytes 184328 | tf_op jit(solution)/shard_map/ppermute | solution.py:69
  25.1 6.8 %collective-permute-done = bf16[24,1280]{1,0:T(8,128)(2,1)S(1)} collective-permute-done((bf16[24,1280]{1,0:T(8,128)(2,1)}, bf16[24,1280]{1,0:T(8,128)(2,1)S(1)}, u32[]{:S(2)}, u32[]{:S(2)}) %collective-permute-start) | collective-permute-done | bytes 61472 | tf_op jit(solution)/shard_map/ppermute | solution.py:69
  32.8 2.8 %collective-permute-start.2 = (bf16[72,1280]{1,0:T(8,128)(2,1)S(1)}, bf16[72,1280]{1,0:T(8,128)(2,1)S(1)}, u32[]{:S(2)}, u32[]{:S(2)}) collective-permute-start(bf16[72,1280]{1,0:T(8,128)(2,1)S(1)} %pad_maximum_fusion.4), channel_id=1, source_target_pairs={{0,3},{1,4},{2,5},{3,6},{4,7},{5,0},{6,1},{7,2},{8,11},{9,12},{10,... | collective-permute-start | bytes 552968 | tf_op jit(solution)/shard_map/ppermute | solution.py:69
  35.6 6.0 %collective-permute-start.3 = (bf16[72,1280]{1,0:T(8,128)(2,1)S(1)}, bf16[72,1280]{1,0:T(8,128)(2,1)S(1)}, u32[]{:S(2)}, u32[]{:S(2)}) collective-permute-start(bf16[72,1280]{1,0:T(8,128)(2,1)S(1)} %pad_maximum_fusion.4), channel_id=1, source_target_pairs={{0,5},{1,6},{2,7},{3,0},{4,1},{5,2},{6,3},{7,4},{8,13},{9,14},{10,... | collective-permute-start | bytes 552968 | tf_op jit(solution)/shard_map/ppermute | solution.py:69
  42.6 4.8 %all-to-all-start.1 = ((bf16[4,96,1152]{2,1,0:T(8,128)(2,1)}), bf16[4,96,1152]{2,1,0:T(8,128)(2,1)S(1)}, u32[]{:S(2)}, u32[]{:S(2)}) async-start(bf16[4,96,1152]{2,1,0:T(8,128)(2,1)} %broadcast_in_dim.2), calls=%async_computation.1 | async-start | bytes 1769472 | tf_op jit(solution)/shard_map/all_to_all | solution.py:48
  50.3 5.8 %collective-permute-start.4 = (bf16[184,1280]{1,0:T(8,128)(2,1)S(1)}, bf16[184,1280]{1,0:T(8,128)(2,1)S(1)}, u32[]{:S(2)}, u32[]{:S(2)}) collective-permute-start(bf16[184,1280]{1,0:T(8,128)(2,1)S(1)} %slice.98), channel_id=1, source_target_pairs={{0,7},{1,0},{2,1},{3,2},{4,3},{5,4},{6,5},{7,6},{8,15},{9,8},{10,9... | collective-permute-start | bytes 1413128 | tf_op jit(solution)/shard_map/ppermute | solution.py:69
  58.2 1.9 %collective-permute-start.6 = (bf16[384,1152]{1,0:T(8,128)(2,1)S(1)}, bf16[384,1152]{1,0:T(8,128)(2,1)}, u32[]{:S(2)}, u32[]{:S(2)}) collective-permute-start(bf16[384,1152]{1,0:T(8,128)(2,1)S(1)} %bitcast.8), channel_id=1, source_target_pairs={{0,24},{24,0},{1,25},{25,1},{2,26},{26,2},{3,27},{27,3},{4,28},{28... | collective-permute-start | bytes 2654216 | tf_op jit(solution)/shard_map/ppermute | solution.py:69
  61.6 2.4 %collective-permute-done.4 = bf16[184,1280]{1,0:T(8,128)(2,1)S(1)} collective-permute-done((bf16[184,1280]{1,0:T(8,128)(2,1)S(1)}, bf16[184,1280]{1,0:T(8,128)(2,1)S(1)}, u32[]{:S(2)}, u32[]{:S(2)}) %collective-permute-start.4) | collective-permute-done | bytes 471072 | tf_op jit(solution)/shard_map/ppermute | solution.py:69
  68.5 3.1 %subtract_convert_fusion = bf16[576,768]{1,0:T(8,128)(2,1)S(1)} fusion(bf16[576,1280]{1,0:T(8,128)(2,1)} %constant_dynamic-update-slice_fusion.3, s32[768]{0:T(1024)S(1)} %add.194, f32[]{:T(128)} %bitcast.7, f32[]{:T(128)} %bitcast, s32[576]{0:T(1024)S(1)} %fusion.15, bf16[384,1152]{1,0:T(8,128)(2,1)} %collective-permute-done.6, ...), kind=kOutput, calls=%fused_computation.5 | convolution fusion | flops 1026736128 | bytes 3987712 | tf_op jit(solution)/shard_map/dot_general | solution.py:111
  71.6 2.1 %convolution_convert_fusion.1 = bf16[360,1152]{1,0:T(8,128)(2,1)S(1)} fusion(bf16[576,768]{1,0:T(8,128)(2,1)S(1)} %subtract_convert_fusion, bf16[384,1152]{1,0:T(8,128)(2,1)} %collective-permute-done.6, bf16[384,1152]{1,0:T(8,128)(2,1)S(1)} %bitcast.10), kind=kOutput, calls=%fused_computation.3 | convolution fusion | flops 640963584 | bytes 3151872 | tf_op jit(solution)/shard_map/dot_general | solution.py:118
  73.8 3.9 %collective-permute-start.8 = (bf16[176,1152]{1,0:T(8,128)(2,1)S(1)}, bf16[176,1152]{1,0:T(8,128)(2,1)S(1)}, u32[]{:S(2)}, u32[]{:S(2)}) collective-permute-start(bf16[176,1152]{1,0:T(8,128)(2,1)S(1)} %slice.85), channel_id=1, source_target_pairs={{0,7},{1,0},{2,1},{3,2},{4,3},{5,4},{6,5},{7,6},{8,15},{9,8},{10,9... | collective-permute-start | bytes 1216520 | tf_op jit(solution)/shard_map/ppermute | solution.py:69
  79.6 2.3 %convolution_convert_fusion = bf16[384,1152]{1,0:T(8,128)(2,1)S(1)} fusion(bf16[576,1280]{1,0:T(8,128)(2,1)} %constant_dynamic-update-slice_fusion.3, bf16[576,768]{1,0:T(8,128)(2,1)S(1)} %subtract_convert_fusion), kind=kOutput, calls=%fused_computation.2 | convolution fusion | flops 510050304 | bytes 2654208 | tf_op jit(solution)/shard_map/dot_general | solution.py:116
  85.7 4.4 %collective-permute-done.7 = bf16[184,1152]{1,0:T(8,128)(2,1)S(1)} collective-permute-done((bf16[184,1152]{1,0:T(8,128)(2,1)S(1)}, bf16[184,1152]{1,0:T(8,128)(2,1)S(1)}, u32[]{:S(2)}, u32[]{:S(2)}) %collective-permute-start.7) | collective-permute-done | bytes 423968 | tf_op jit(solution)/shard_map/ppermute | solution.py:69
  91.1 3.6 %collective-permute-start.9 = (bf16[72,1152]{1,0:T(8,128)(2,1)}, bf16[72,1152]{1,0:T(8,128)(2,1)}, u32[]{:S(2)}, u32[]{:S(2)}) collective-permute-start(bf16[72,1152]{1,0:T(8,128)(2,1)} %get-tuple-element.20), channel_id=1, source_target_pairs={{0,5},{1,6},{2,7},{3,0},{4,1},{5,2},{6,3},{7,4},{8,13},{9,14},{10,... | collective-permute-start | bytes 497672 | tf_op jit(solution)/shard_map/ppermute | solution.py:69
  94.6 5.3 %collective-permute-start.10 = (bf16[72,1152]{1,0:T(8,128)(2,1)}, bf16[72,1152]{1,0:T(8,128)(2,1)}, u32[]{:S(2)}, u32[]{:S(2)}) collective-permute-start(bf16[72,1152]{1,0:T(8,128)(2,1)} %get-tuple-element.21), channel_id=1, source_target_pairs={{0,3},{1,4},{2,5},{3,6},{4,7},{5,0},{6,1},{7,2},{8,11},{9,12},{10,... | collective-permute-start | bytes 497672 | tf_op jit(solution)/shard_map/ppermute | solution.py:69
  99.9 3.2 %fusion = bf16[384,1152]{1,0:T(8,128)(2,1)} fusion(bf16[384,1152]{1,0:T(8,128)(2,1)S(1)} %collective-permute-done.13, bf16[576,1280]{1,0:T(8,128)(2,1)} %constant_dynamic-update-slice_fusion.3, bf16[576,768]{1,0:T(8,128)(2,1)S(1)} %subtract_convert_fusion), kind=kOutput, calls=%fused_computation.1 | convolution fusion | flops 510935040 | bytes 3538944 | tf_op jit(solution)/shard_map/dot_general | solution.py:116
  103.1 4.8 %all-to-all-start.2 = ((bf16[4,96,1152]{2,1,0:T(8,128)(2,1)}), bf16[4,96,1152]{2,1,0:T(8,128)(2,1)S(1)}, u32[]{:S(2)}, u32[]{:S(2)}) async-start(bf16[4,96,1152]{2,1,0:T(8,128)(2,1)} %bitcast.12), calls=%async_computation.2 | async-start | bytes 1769472 | tf_op jit(solution)/shard_map/all_to_all | solution.py:48
  107.9 4.3 %collective-permute-done.10 = bf16[72,1152]{1,0:T(8,128)(2,1)} collective-permute-done((bf16[72,1152]{1,0:T(8,128)(2,1)}, bf16[72,1152]{1,0:T(8,128)(2,1)}, u32[]{:S(2)}, u32[]{:S(2)}) %collective-permute-start.10) | collective-permute-done | bytes 165920 | tf_op jit(solution)/shard_map/ppermute | solution.py:69
  114.0 6.3 %collective-permute-start.11 = (bf16[24,1152]{1,0:T(8,128)(2,1)S(1)}, bf16[24,1152]{1,0:T(8,128)(2,1)S(1)}, u32[]{:S(2)}, u32[]{:S(2)}) collective-permute-start(bf16[24,1152]{1,0:T(8,128)(2,1)S(1)} %get-tuple-element.28), channel_id=1, source_target_pairs={{0,200},{8,208},{16,384},{192,392},{200,400},{208,576},{384,584},{... | collective-permute-start | bytes 165896 | tf_op jit(solution)/shard_map/ppermute | solution.py:69
  120.3 3.6 %collective-permute-start.12 = (bf16[24,1152]{1,0:T(8,128)(2,1)S(1)}, bf16[24,1152]{1,0:T(8,128)(2,1)S(1)}, u32[]{:S(2)}, u32[]{:S(2)}) collective-permute-start(bf16[24,1152]{1,0:T(8,128)(2,1)S(1)} %get-tuple-element.29), channel_id=1, source_target_pairs={{0,400},{8,576},{16,584},{192,592},{200,0},{208,8},{384,16},{392,1... | collective-permute-start | bytes 165896 | tf_op jit(solution)/shard_map/ppermute | solution.py:69
  125.7 5.9 %all-to-all-start.3 = ((bf16[4,24,1152]{2,1,0:T(8,128)(2,1)}), bf16[4,24,1152]{2,1,0:T(8,128)(2,1)S(1)}, u32[]{:S(2)}, u32[]{:S(2)}) async-start(bf16[4,24,1152]{2,1,0:T(8,128)(2,1)} %bitcast.6), calls=%async_computation.3 | async-start | bytes 442368 | tf_op jit(solution)/shard_map/all_to_all | solution.py:48
  132.6 6.7 %all-to-all-done.3 = bf16[4,24,1152]{2,1,0:T(8,128)(2,1)S(1)} async-done(((bf16[4,24,1152]{2,1,0:T(8,128)(2,1)}), bf16[4,24,1152]{2,1,0:T(8,128)(2,1)S(1)}, u32[]{:S(2)}, u32[]{:S(2)}) %all-to-all-start.3) | async-done | bytes 221216 | tf_op jit(solution)/shard_map/all_to_all | solution.py:48
  (57 shorter events, 27.1 us)
Async XLA Ops:
  2.3 30.5 %all-to-all-start = ((bf16[4,24,1152]{2,1,0:T(8,128)(2,1)}), bf16[4,24,1152]{2,1,0:T(8,128)(2,1)S(1)}, u32[]{:S(2)}, u32[]{:S(2)}) async-start(bf16[4,24,1152]{2,1,0:T(8,128)(2,1)} %get-tuple-element.11), calls=%async_computation | async-start | bytes 442368 | tf_op jit(solution)/shard_map/all_to_all | solution.py:48
  9.6 15.5 %collective-permute-start.1 = (bf16[24,1280]{1,0:T(8,128)(2,1)}, bf16[24,1280]{1,0:T(8,128)(2,1)S(1)}, u32[]{:S(2)}, u32[]{:S(2)}) collective-permute-start(bf16[24,1280]{1,0:T(8,128)(2,1)} %get-tuple-element.10), channel_id=1, source_target_pairs={{0,200},{8,208},{16,384},{192,392},{200,400},{208,576},{384,584},{... | collective-permute-start | bytes 184328 | tf_op jit(solution)/shard_map/ppermute | solution.py:69
  20.2 11.8 %collective-permute-start = (bf16[24,1280]{1,0:T(8,128)(2,1)}, bf16[24,1280]{1,0:T(8,128)(2,1)S(1)}, u32[]{:S(2)}, u32[]{:S(2)}) collective-permute-start(bf16[24,1280]{1,0:T(8,128)(2,1)} %get-tuple-element.10), channel_id=1, source_target_pairs={{0,400},{8,576},{16,584},{192,592},{200,0},{208,8},{384,16},{392,1... | collective-permute-start | bytes 184328 | tf_op jit(solution)/shard_map/ppermute | solution.py:69
  32.8 14.6 %collective-permute-start.2 = (bf16[72,1280]{1,0:T(8,128)(2,1)S(1)}, bf16[72,1280]{1,0:T(8,128)(2,1)S(1)}, u32[]{:S(2)}, u32[]{:S(2)}) collective-permute-start(bf16[72,1280]{1,0:T(8,128)(2,1)S(1)} %pad_maximum_fusion.4), channel_id=1, source_target_pairs={{0,3},{1,4},{2,5},{3,6},{4,7},{5,0},{6,1},{7,2},{8,11},{9,12},{10,... | collective-permute-start | bytes 552968 | tf_op jit(solution)/shard_map/ppermute | solution.py:69
  35.6 14.0 %collective-permute-start.3 = (bf16[72,1280]{1,0:T(8,128)(2,1)S(1)}, bf16[72,1280]{1,0:T(8,128)(2,1)S(1)}, u32[]{:S(2)}, u32[]{:S(2)}) collective-permute-start(bf16[72,1280]{1,0:T(8,128)(2,1)S(1)} %pad_maximum_fusion.4), channel_id=1, source_target_pairs={{0,5},{1,6},{2,7},{3,0},{4,1},{5,2},{6,3},{7,4},{8,13},{9,14},{10,... | collective-permute-start | bytes 552968 | tf_op jit(solution)/shard_map/ppermute | solution.py:69
  42.6 15.5 %all-to-all-start.1 = ((bf16[4,96,1152]{2,1,0:T(8,128)(2,1)}), bf16[4,96,1152]{2,1,0:T(8,128)(2,1)S(1)}, u32[]{:S(2)}, u32[]{:S(2)}) async-start(bf16[4,96,1152]{2,1,0:T(8,128)(2,1)} %broadcast_in_dim.2), calls=%async_computation.1 | async-start | bytes 1769472 | tf_op jit(solution)/shard_map/all_to_all | solution.py:48
  50.3 13.6 %collective-permute-start.4 = (bf16[184,1280]{1,0:T(8,128)(2,1)S(1)}, bf16[184,1280]{1,0:T(8,128)(2,1)S(1)}, u32[]{:S(2)}, u32[]{:S(2)}) collective-permute-start(bf16[184,1280]{1,0:T(8,128)(2,1)S(1)} %slice.98), channel_id=1, source_target_pairs={{0,7},{1,0},{2,1},{3,2},{4,3},{5,4},{6,5},{7,6},{8,15},{9,8},{10,9... | collective-permute-start | bytes 1413128 | tf_op jit(solution)/shard_map/ppermute | solution.py:69
  56.2 10.3 %collective-permute-start.5 = (bf16[176,1280]{1,0:T(8,128)(2,1)S(1)}, bf16[176,1280]{1,0:T(8,128)(2,1)S(1)}, u32[]{:S(2)}, u32[]{:S(2)}) collective-permute-start(bf16[176,1280]{1,0:T(8,128)(2,1)S(1)} %slice.99), channel_id=1, source_target_pairs={{0,1},{1,2},{2,3},{3,4},{4,5},{5,6},{6,7},{7,0},{8,9},{9,10},{10,1... | collective-permute-start | bytes 1351688 | tf_op jit(solution)/shard_map/ppermute | solution.py:69
  58.2 10.4 %collective-permute-start.6 = (bf16[384,1152]{1,0:T(8,128)(2,1)S(1)}, bf16[384,1152]{1,0:T(8,128)(2,1)}, u32[]{:S(2)}, u32[]{:S(2)}) collective-permute-start(bf16[384,1152]{1,0:T(8,128)(2,1)S(1)} %bitcast.8), channel_id=1, source_target_pairs={{0,24},{24,0},{1,25},{25,1},{2,26},{26,2},{3,27},{27,3},{4,28},{28... | collective-permute-start | bytes 2654216 | tf_op jit(solution)/shard_map/ppermute | solution.py:69
  73.8 11.8 %collective-permute-start.8 = (bf16[176,1152]{1,0:T(8,128)(2,1)S(1)}, bf16[176,1152]{1,0:T(8,128)(2,1)S(1)}, u32[]{:S(2)}, u32[]{:S(2)}) collective-permute-start(bf16[176,1152]{1,0:T(8,128)(2,1)S(1)} %slice.85), channel_id=1, source_target_pairs={{0,7},{1,0},{2,1},{3,2},{4,3},{5,4},{6,5},{7,6},{8,15},{9,8},{10,9... | collective-permute-start | bytes 1216520 | tf_op jit(solution)/shard_map/ppermute | solution.py:69
  77.7 12.4 %collective-permute-start.7 = (bf16[184,1152]{1,0:T(8,128)(2,1)S(1)}, bf16[184,1152]{1,0:T(8,128)(2,1)S(1)}, u32[]{:S(2)}, u32[]{:S(2)}) collective-permute-start(bf16[184,1152]{1,0:T(8,128)(2,1)S(1)} %slice.83), channel_id=1, source_target_pairs={{0,1},{1,2},{2,3},{3,4},{4,5},{5,6},{6,7},{7,0},{8,9},{9,10},{10,1... | collective-permute-start | bytes 1271816 | tf_op jit(solution)/shard_map/ppermute | solution.py:69
  81.9 18.0 %collective-permute-start.13 = (bf16[384,1152]{1,0:T(8,128)(2,1)S(1)}, bf16[384,1152]{1,0:T(8,128)(2,1)S(1)}, u32[]{:S(2)}, u32[]{:S(2)}) collective-permute-start(bf16[384,1152]{1,0:T(8,128)(2,1)S(1)} %convolution_convert_fusion), channel_id=1, source_target_pairs={{0,24},{24,0},{1,25},{25,1},{2,26},{26,2},{3,27},{27,3},{4,28},{28... | collective-permute-start | bytes 2654216 | tf_op jit(solution)/shard_map/ppermute | solution.py:69
  91.1 16.8 %collective-permute-start.9 = (bf16[72,1152]{1,0:T(8,128)(2,1)}, bf16[72,1152]{1,0:T(8,128)(2,1)}, u32[]{:S(2)}, u32[]{:S(2)}) collective-permute-start(bf16[72,1152]{1,0:T(8,128)(2,1)} %get-tuple-element.20), channel_id=1, source_target_pairs={{0,5},{1,6},{2,7},{3,0},{4,1},{5,2},{6,3},{7,4},{8,13},{9,14},{10,... | collective-permute-start | bytes 497672 | tf_op jit(solution)/shard_map/ppermute | solution.py:69
  94.6 17.6 %collective-permute-start.10 = (bf16[72,1152]{1,0:T(8,128)(2,1)}, bf16[72,1152]{1,0:T(8,128)(2,1)}, u32[]{:S(2)}, u32[]{:S(2)}) collective-permute-start(bf16[72,1152]{1,0:T(8,128)(2,1)} %get-tuple-element.21), channel_id=1, source_target_pairs={{0,3},{1,4},{2,5},{3,6},{4,7},{5,0},{6,1},{7,2},{8,11},{9,12},{10,... | collective-permute-start | bytes 497672 | tf_op jit(solution)/shard_map/ppermute | solution.py:69
  103.1 21.8 %all-to-all-start.2 = ((bf16[4,96,1152]{2,1,0:T(8,128)(2,1)}), bf16[4,96,1152]{2,1,0:T(8,128)(2,1)S(1)}, u32[]{:S(2)}, u32[]{:S(2)}) async-start(bf16[4,96,1152]{2,1,0:T(8,128)(2,1)} %bitcast.12), calls=%async_computation.2 | async-start | bytes 1769472 | tf_op jit(solution)/shard_map/all_to_all | solution.py:48
  107.9 16.9 %copy-start.3 = (f32[24,1]{1,0:T(8,128)S(1)}, f32[24,1]{1,0:T(8,128)}, u32[]{:S(2)}) copy-start(f32[24,1]{1,0:T(8,128)} %get-tuple-element.17) | copy-start | bytes 292
  114.0 17.6 %copy-start = (f32[72,1152]{1,0:T(8,128)S(1)}, f32[72,1152]{1,0:T(8,128)}, u32[]{:S(2)}) copy-start(f32[72,1152]{1,0:T(8,128)} %get-tuple-element.19) | copy-start | bytes 995332
  114.0 17.6 %copy-start.1 = (bf16[24,1152]{1,0:T(8,128)(2,1)S(1)}, bf16[24,1152]{1,0:T(8,128)(2,1)}, u32[]{:S(2)}) copy-start(bf16[24,1152]{1,0:T(8,128)(2,1)} %img_ref.1) | copy-start | bytes 165892
  114.0 25.3 %copy-start.2 = (bf16[24,1152]{1,0:T(8,128)(2,1)S(1)}, bf16[24,1152]{1,0:T(8,128)(2,1)}, u32[]{:S(2)}) copy-start(bf16[24,1152]{1,0:T(8,128)(2,1)} %txt_ref.1) | copy-start | bytes 165892
  114.0 17.6 %collective-permute-start.11 = (bf16[24,1152]{1,0:T(8,128)(2,1)S(1)}, bf16[24,1152]{1,0:T(8,128)(2,1)S(1)}, u32[]{:S(2)}, u32[]{:S(2)}) collective-permute-start(bf16[24,1152]{1,0:T(8,128)(2,1)S(1)} %get-tuple-element.28), channel_id=1, source_target_pairs={{0,200},{8,208},{16,384},{192,392},{200,400},{208,576},{384,584},{... | collective-permute-start | bytes 165896 | tf_op jit(solution)/shard_map/ppermute | solution.py:69
  120.3 11.3 %collective-permute-start.12 = (bf16[24,1152]{1,0:T(8,128)(2,1)S(1)}, bf16[24,1152]{1,0:T(8,128)(2,1)S(1)}, u32[]{:S(2)}, u32[]{:S(2)}) collective-permute-start(bf16[24,1152]{1,0:T(8,128)(2,1)S(1)} %get-tuple-element.29), channel_id=1, source_target_pairs={{0,400},{8,576},{16,584},{192,592},{200,0},{208,8},{384,16},{392,1... | collective-permute-start | bytes 165896 | tf_op jit(solution)/shard_map/ppermute | solution.py:69
  125.7 13.5 %all-to-all-start.3 = ((bf16[4,24,1152]{2,1,0:T(8,128)(2,1)}), bf16[4,24,1152]{2,1,0:T(8,128)(2,1)S(1)}, u32[]{:S(2)}, u32[]{:S(2)}) async-start(bf16[4,24,1152]{2,1,0:T(8,128)(2,1)} %bitcast.6), calls=%async_computation.3 | async-start | bytes 442368 | tf_op jit(solution)/shard_map/all_to_all | solution.py:48

commit v6 on v5

--- a/solution.py
+++ b/solution.py
@@ -131,6 +131,7 @@
     mid = mine[y : 2 * y] + before[y : 2 * y] + after[rest : rest + y]
     top = mine[2 * y :] + jnp.pad(before[2 * y :], ((0, rest), (0, 0))) + after[rest + y :]
     mid = mid + send(low, "y", -3).astype(F32) + send(top, "y", 3).astype(F32)
+    mid, txt_sum = lax.optimization_barrier((mid, txt_sum))
     one, two = send(mid[blk : 2 * blk], Z, RUN), send(mid[2 * blk :], Z, -RUN)
     img_sum = mid[:blk] + one.astype(F32) + two.astype(F32)
     return (

time: 141 us -> 154 us (1.092)
  the two profiles are of different devices: /device:TPU:54 before, /device:TPU:10 now
where the time goes in v6:
time: 154 us; the launch traced here: 152 us
  starting transfers between devices  80 us (52%)
  waiting for transfers between devices  43.9 us (29%)
  matrix products  9.83 us (6%)
  other arithmetic  9.41 us (6%)
  local copies, waits for them, and re-layouts  5.38 us (3%)
  between operations  2.33 us (2%)
  Pallas kernels  1.66 us (1%)
    ppermute x14, starting transfers between devices, send(): lax.ppermute(x.astype(BF), axis, [(i, (i + hop) % size) for i in range(si...  58.7 us
    ppermute x14, waiting for transfers between devices, send(): lax.ppermute(x.astype(BF), axis, [(i, (i + hop) % size) for i in range(si...  43.9 us
    all_to_all x4, starting transfers between devices, exchange(): lax.all_to_all(blocks, axes, split_axis=0, concat_axis=0, axis_index_grou...  21.3 us
    dot_general x1, matrix products, on_device(): lax.dot_general(img, txt, (((1,), (1,)), ((), ())), preferred_element_typ...  3.09 us
  transfers between devices with their start and end apart: 18, of which 9 were waited for; matrix products, arithmetic and copies ran while one was open for 9% of the time, Pallas kernels for 0%

profile of v6, /device:TPU:10, one launch (start us, length us, event | category | flops | bytes accessed | tf_op | source)
XLA Modules:
  0.0 152.5 jit_solution(1781621206670321031)
XLA Ops:
  2.3 7.3 %all-to-all-start = ((bf16[4,24,1152]{2,1,0:T(8,128)(2,1)}), bf16[4,24,1152]{2,1,0:T(8,128)(2,1)S(1)}, u32[]{:S(2)}, u32[]{:S(2)}) async-start(bf16[4,24,1152]{2,1,0:T(8,128)(2,1)} %get-tuple-element.13), calls=%async_computation | async-start | bytes 442368 | tf_op jit(solution)/shard_map/all_to_all | solution.py:48
  9.5 10.6 %collective-permute-start.1 = (bf16[24,1280]{1,0:T(8,128)(2,1)}, bf16[24,1280]{1,0:T(8,128)(2,1)S(1)}, u32[]{:S(2)}, u32[]{:S(2)}) collective-permute-start(bf16[24,1280]{1,0:T(8,128)(2,1)} %get-tuple-element.12), channel_id=1, source_target_pairs={{0,200},{8,208},{16,384},{192,392},{200,400},{208,576},{384,584},{... | collective-permute-start | bytes 184328 | tf_op jit(solution)/shard_map/ppermute | solution.py:69
  20.2 3.2 %collective-permute-start = (bf16[24,1280]{1,0:T(8,128)(2,1)}, bf16[24,1280]{1,0:T(8,128)(2,1)S(1)}, u32[]{:S(2)}, u32[]{:S(2)}) collective-permute-start(bf16[24,1280]{1,0:T(8,128)(2,1)} %get-tuple-element.12), channel_id=1, source_target_pairs={{0,400},{8,576},{16,584},{192,592},{200,0},{208,8},{384,16},{392,1... | collective-permute-start | bytes 184328 | tf_op jit(solution)/shard_map/ppermute | solution.py:69
  25.1 6.8 %collective-permute-done = bf16[24,1280]{1,0:T(8,128)(2,1)S(1)} collective-permute-done((bf16[24,1280]{1,0:T(8,128)(2,1)}, bf16[24,1280]{1,0:T(8,128)(2,1)S(1)}, u32[]{:S(2)}, u32[]{:S(2)}) %collective-permute-start) | collective-permute-done | bytes 61472 | tf_op jit(solution)/shard_map/ppermute | solution.py:69
  32.8 6.7 %collective-permute-start.2 = (bf16[72,1280]{1,0:T(8,128)(2,1)S(1)}, bf16[72,1280]{1,0:T(8,128)(2,1)S(1)}, u32[]{:S(2)}, u32[]{:S(2)}) collective-permute-start(bf16[72,1280]{1,0:T(8,128)(2,1)S(1)} %pad_maximum_fusion.4), channel_id=1, source_target_pairs={{0,3},{1,4},{2,5},{3,6},{4,7},{5,0},{6,1},{7,2},{8,11},{9,12},{10,... | collective-permute-start | bytes 552968 | tf_op jit(solution)/shard_map/ppermute | solution.py:69
  39.5 2.1 %collective-permute-start.3 = (bf16[72,1280]{1,0:T(8,128)(2,1)S(1)}, bf16[72,1280]{1,0:T(8,128)(2,1)S(1)}, u32[]{:S(2)}, u32[]{:S(2)}) collective-permute-start(bf16[72,1280]{1,0:T(8,128)(2,1)S(1)} %pad_maximum_fusion.4), channel_id=1, source_target_pairs={{0,5},{1,6},{2,7},{3,0},{4,1},{5,2},{6,3},{7,4},{8,13},{9,14},{10,... | collective-permute-start | bytes 552968 | tf_op jit(solution)/shard_map/ppermute | solution.py:69
  42.6 4.8 %all-to-all-start.1 = ((bf16[4,96,1152]{2,1,0:T(8,128)(2,1)}), bf16[4,96,1152]{2,1,0:T(8,128)(2,1)S(1)}, u32[]{:S(2)}, u32[]{:S(2)}) async-start(bf16[4,96,1152]{2,1,0:T(8,128)(2,1)} %broadcast_in_dim.2), calls=%async_computation.1 | async-start | bytes 1769472 | tf_op jit(solution)/shard_map/all_to_all | solution.py:48
  48.9 6.5 %collective-permute-done.3 = bf16[72,1280]{1,0:T(8,128)(2,1)S(1)} collective-permute-done((bf16[72,1280]{1,0:T(8,128)(2,1)S(1)}, bf16[72,1280]{1,0:T(8,128)(2,1)S(1)}, u32[]{:S(2)}, u32[]{:S(2)}) %collective-permute-start.3) | collective-permute-done | bytes 184352 | tf_op jit(solution)/shard_map/ppermute | solution.py:69
  56.6 1.9 %collective-permute-start.4 = (bf16[184,1280]{1,0:T(8,128)(2,1)S(1)}, bf16[184,1280]{1,0:T(8,128)(2,1)S(1)}, u32[]{:S(2)}, u32[]{:S(2)}) collective-permute-start(bf16[184,1280]{1,0:T(8,128)(2,1)S(1)} %slice.98), channel_id=1, source_target_pairs={{0,7},{1,0},{2,1},{3,2},{4,3},{5,4},{6,5},{7,6},{8,15},{9,8},{10,9... | collective-permute-start | bytes 1413128 | tf_op jit(solution)/shard_map/ppermute | solution.py:69
  58.6 3.9 %collective-permute-start.5 = (bf16[176,1280]{1,0:T(8,128)(2,1)S(1)}, bf16[176,1280]{1,0:T(8,128)(2,1)S(1)}, u32[]{:S(2)}, u32[]{:S(2)}) collective-permute-start(bf16[176,1280]{1,0:T(8,128)(2,1)S(1)} %slice.99), channel_id=1, source_target_pairs={{0,1},{1,2},{2,3},{3,4},{4,5},{5,6},{6,7},{7,0},{8,9},{9,10},{10,1... | collective-permute-start | bytes 1351688 | tf_op jit(solution)/shard_map/ppermute | solution.py:69
  62.5 1.9 %collective-permute-start.6 = (bf16[384,1152]{1,0:T(8,128)(2,1)S(1)}, bf16[384,1152]{1,0:T(8,128)(2,1)}, u32[]{:S(2)}, u32[]{:S(2)}) collective-permute-start(bf16[384,1152]{1,0:T(8,128)(2,1)S(1)} %bitcast.8), channel_id=1, source_target_pairs={{0,24},{24,0},{1,25},{25,1},{2,26},{26,2},{3,27},{27,3},{4,28},{28... | collective-permute-start | bytes 2654216 | tf_op jit(solution)/shard_map/ppermute | solution.py:69
  70.9 3.1 %subtract_convert_fusion = bf16[576,768]{1,0:T(8,128)(2,1)S(1)} fusion(bf16[576,1280]{1,0:T(8,128)(2,1)} %constant_dynamic-update-slice_fusion.3, s32[768]{0:T(1024)S(1)} %add.194, f32[]{:T(128)} %bitcast.7, f32[]{:T(128)} %bitcast, s32[576]{0:T(1024)S(1)} %fusion.15, bf16[384,1152]{1,0:T(8,128)(2,1)} %collective-permute-done.6, ...), kind=kOutput, calls=%fused_computation.5 | convolution fusion | flops 1026736128 | bytes 3987712 | tf_op jit(solution)/shard_map/dot_general | solution.py:111
  74.0 2.2 %convolution_convert_fusion.1 = bf16[360,1152]{1,0:T(8,128)(2,1)S(1)} fusion(bf16[576,768]{1,0:T(8,128)(2,1)S(1)} %subtract_convert_fusion, bf16[384,1152]{1,0:T(8,128)(2,1)} %collective-permute-done.6, bf16[384,1152]{1,0:T(8,128)(2,1)S(1)} %bitcast.10), kind=kOutput, calls=%fused_computation.3 | convolution fusion | flops 640963584 | bytes 3151872 | tf_op jit(solution)/shard_map/dot_general | solution.py:118
  77.1 1.9 %collective-permute-start.11 = (bf16[384,1152]{1,0:T(8,128)(2,1)S(1)}, bf16[384,1152]{1,0:T(8,128)(2,1)S(1)}, u32[]{:S(2)}, u32[]{:S(2)}) collective-permute-start(bf16[384,1152]{1,0:T(8,128)(2,1)S(1)} %convolution_convert_fusion), channel_id=1, source_target_pairs={{0,24},{24,0},{1,25},{25,1},{2,26},{26,2},{3,27},{27,3},{4,28},{28... | collective-permute-start | bytes 2654216 | tf_op jit(solution)/shard_map/ppermute | solution.py:69
  79.1 3.9 %collective-permute-start.7 = (bf16[184,1152]{1,0:T(8,128)(2,1)S(1)}, bf16[184,1152]{1,0:T(8,128)(2,1)S(1)}, u32[]{:S(2)}, u32[]{:S(2)}) collective-permute-start(bf16[184,1152]{1,0:T(8,128)(2,1)S(1)} %slice.83), channel_id=1, source_target_pairs={{0,1},{1,2},{2,3},{3,4},{4,5},{5,6},{6,7},{7,0},{8,9},{9,10},{10,1... | collective-permute-start | bytes 1271816 | tf_op jit(solution)/shard_map/ppermute | solution.py:69
  83.1 1.9 %collective-permute-start.8 = (bf16[176,1152]{1,0:T(8,128)(2,1)S(1)}, bf16[176,1152]{1,0:T(8,128)(2,1)S(1)}, u32[]{:S(2)}, u32[]{:S(2)}) collective-permute-start(bf16[176,1152]{1,0:T(8,128)(2,1)S(1)} %slice.85), channel_id=1, source_target_pairs={{0,7},{1,0},{2,1},{3,2},{4,3},{5,4},{6,5},{7,6},{8,15},{9,8},{10,9... | collective-permute-start | bytes 1216520 | tf_op jit(solution)/shard_map/ppermute | solution.py:69
  86.8 9.7 %collective-permute-done.8 = bf16[176,1152]{1,0:T(8,128)(2,1)S(1)} collective-permute-done((bf16[176,1152]{1,0:T(8,128)(2,1)S(1)}, bf16[176,1152]{1,0:T(8,128)(2,1)S(1)}, u32[]{:S(2)}, u32[]{:S(2)}) %collective-permute-start.8) | collective-permute-done | bytes 405536 | tf_op jit(solution)/shard_map/ppermute | solution.py:69
  99.8 5.0 %all-to-all-start.2 = ((bf16[4,96,1152]{2,1,0:T(8,128)(2,1)}), bf16[4,96,1152]{2,1,0:T(8,128)(2,1)S(1)}, u32[]{:S(2)}, u32[]{:S(2)}) async-start(bf16[4,96,1152]{2,1,0:T(8,128)(2,1)} %bitcast.12), calls=%async_computation.2 | async-start | bytes 1769472 | tf_op jit(solution)/shard_map/all_to_all | solution.py:48
  106.6 2.8 %collective-permute-start.9 = (bf16[72,1152]{1,0:T(8,128)(2,1)}, bf16[72,1152]{1,0:T(8,128)(2,1)}, u32[]{:S(2)}, u32[]{:S(2)}) collective-permute-start(bf16[72,1152]{1,0:T(8,128)(2,1)} %get-tuple-element.22), channel_id=1, source_target_pairs={{0,5},{1,6},{2,7},{3,0},{4,1},{5,2},{6,3},{7,4},{8,13},{9,14},{10,... | collective-permute-start | bytes 497672 | tf_op jit(solution)/shard_map/ppermute | solution.py:69
  109.5 6.0 %collective-permute-start.10 = (bf16[72,1152]{1,0:T(8,128)(2,1)}, bf16[72,1152]{1,0:T(8,128)(2,1)}, u32[]{:S(2)}, u32[]{:S(2)}) collective-permute-start(bf16[72,1152]{1,0:T(8,128)(2,1)} %get-tuple-element.23), channel_id=1, source_target_pairs={{0,3},{1,4},{2,5},{3,6},{4,7},{5,0},{6,1},{7,2},{8,11},{9,12},{10,... | collective-permute-start | bytes 497672 | tf_op jit(solution)/shard_map/ppermute | solution.py:69
  117.8 4.3 %all-to-all-start.3 = ((bf16[4,24,1152]{2,1,0:T(8,128)(2,1)}), bf16[4,24,1152]{2,1,0:T(8,128)(2,1)S(1)}, u32[]{:S(2)}, u32[]{:S(2)}) async-start(bf16[4,24,1152]{2,1,0:T(8,128)(2,1)} %bitcast.14), calls=%async_computation.3 | async-start | bytes 442368 | tf_op jit(solution)/shard_map/all_to_all | solution.py:48
  122.1 5.7 %collective-permute-done.10 = bf16[72,1152]{1,0:T(8,128)(2,1)} collective-permute-done((bf16[72,1152]{1,0:T(8,128)(2,1)}, bf16[72,1152]{1,0:T(8,128)(2,1)}, u32[]{:S(2)}, u32[]{:S(2)}) %collective-permute-start.10) | collective-permute-done | bytes 165920 | tf_op jit(solution)/shard_map/ppermute | solution.py:69
  129.0 9.7 %collective-permute-start.12 = (bf16[24,1152]{1,0:T(8,128)(2,1)S(1)}, bf16[24,1152]{1,0:T(8,128)(2,1)S(1)}, u32[]{:S(2)}, u32[]{:S(2)}) collective-permute-start(bf16[24,1152]{1,0:T(8,128)(2,1)S(1)} %get-tuple-element.30), channel_id=1, source_target_pairs={{0,200},{8,208},{16,384},{192,392},{200,400},{208,576},{384,584},{... | collective-permute-start | bytes 165896 | tf_op jit(solution)/shard_map/ppermute | solution.py:69
  141.6 9.9 %collective-permute-done.13 = bf16[24,1152]{1,0:T(8,128)(2,1)S(1)} collective-permute-done((bf16[24,1152]{1,0:T(8,128)(2,1)S(1)}, bf16[24,1152]{1,0:T(8,128)(2,1)S(1)}, u32[]{:S(2)}, u32[]{:S(2)}) %collective-permute-start.13) | collective-permute-done | bytes 55328 | tf_op jit(solution)/shard_map/ppermute | solution.py:69
  (62 shorter events, 28.2 us)
Async XLA Ops:
  2.3 30.5 %all-to-all-start = ((bf16[4,24,1152]{2,1,0:T(8,128)(2,1)}), bf16[4,24,1152]{2,1,0:T(8,128)(2,1)S(1)}, u32[]{:S(2)}, u32[]{:S(2)}) async-start(bf16[4,24,1152]{2,1,0:T(8,128)(2,1)} %get-tuple-element.13), calls=%async_computation | async-start | bytes 442368 | tf_op jit(solution)/shard_map/all_to_all | solution.py:48
  9.5 15.5 %collective-permute-start.1 = (bf16[24,1280]{1,0:T(8,128)(2,1)}, bf16[24,1280]{1,0:T(8,128)(2,1)S(1)}, u32[]{:S(2)}, u32[]{:S(2)}) collective-permute-start(bf16[24,1280]{1,0:T(8,128)(2,1)} %get-tuple-element.12), channel_id=1, source_target_pairs={{0,200},{8,208},{16,384},{192,392},{200,400},{208,576},{384,584},{... | collective-permute-start | bytes 184328 | tf_op jit(solution)/shard_map/ppermute | solution.py:69
  20.2 11.8 %collective-permute-start = (bf16[24,1280]{1,0:T(8,128)(2,1)}, bf16[24,1280]{1,0:T(8,128)(2,1)S(1)}, u32[]{:S(2)}, u32[]{:S(2)}) collective-permute-start(bf16[24,1280]{1,0:T(8,128)(2,1)} %get-tuple-element.12), channel_id=1, source_target_pairs={{0,400},{8,576},{16,584},{192,592},{200,0},{208,8},{384,16},{392,1... | collective-permute-start | bytes 184328 | tf_op jit(solution)/shard_map/ppermute | solution.py:69
  32.8 16.1 %collective-permute-start.2 = (bf16[72,1280]{1,0:T(8,128)(2,1)S(1)}, bf16[72,1280]{1,0:T(8,128)(2,1)S(1)}, u32[]{:S(2)}, u32[]{:S(2)}) collective-permute-start(bf16[72,1280]{1,0:T(8,128)(2,1)S(1)} %pad_maximum_fusion.4), channel_id=1, source_target_pairs={{0,3},{1,4},{2,5},{3,6},{4,7},{5,0},{6,1},{7,2},{8,11},{9,12},{10,... | collective-permute-start | bytes 552968 | tf_op jit(solution)/shard_map/ppermute | solution.py:69
  39.5 15.9 %collective-permute-start.3 = (bf16[72,1280]{1,0:T(8,128)(2,1)S(1)}, bf16[72,1280]{1,0:T(8,128)(2,1)S(1)}, u32[]{:S(2)}, u32[]{:S(2)}) collective-permute-start(bf16[72,1280]{1,0:T(8,128)(2,1)S(1)} %pad_maximum_fusion.4), channel_id=1, source_target_pairs={{0,5},{1,6},{2,7},{3,0},{4,1},{5,2},{6,3},{7,4},{8,13},{9,14},{10,... | collective-permute-start | bytes 552968 | tf_op jit(solution)/shard_map/ppermute | solution.py:69
  42.6 19.9 %all-to-all-start.1 = ((bf16[4,96,1152]{2,1,0:T(8,128)(2,1)}), bf16[4,96,1152]{2,1,0:T(8,128)(2,1)S(1)}, u32[]{:S(2)}, u32[]{:S(2)}) async-start(bf16[4,96,1152]{2,1,0:T(8,128)(2,1)} %broadcast_in_dim.2), calls=%async_computation.1 | async-start | bytes 1769472 | tf_op jit(solution)/shard_map/all_to_all | solution.py:48
  55.4 1.1 copy-start.2
  56.6 10.5 %collective-permute-start.4 = (bf16[184,1280]{1,0:T(8,128)(2,1)S(1)}, bf16[184,1280]{1,0:T(8,128)(2,1)S(1)}, u32[]{:S(2)}, u32[]{:S(2)}) collective-permute-start(bf16[184,1280]{1,0:T(8,128)(2,1)S(1)} %slice.98), channel_id=1, source_target_pairs={{0,7},{1,0},{2,1},{3,2},{4,3},{5,4},{6,5},{7,6},{8,15},{9,8},{10,9... | collective-permute-start | bytes 1413128 | tf_op jit(solution)/shard_map/ppermute | solution.py:69
  58.6 10.3 %collective-permute-start.5 = (bf16[176,1280]{1,0:T(8,128)(2,1)S(1)}, bf16[176,1280]{1,0:T(8,128)(2,1)S(1)}, u32[]{:S(2)}, u32[]{:S(2)}) collective-permute-start(bf16[176,1280]{1,0:T(8,128)(2,1)S(1)} %slice.99), channel_id=1, source_target_pairs={{0,1},{1,2},{2,3},{3,4},{4,5},{5,6},{6,7},{7,0},{8,9},{9,10},{10,1... | collective-permute-start | bytes 1351688 | tf_op jit(solution)/shard_map/ppermute | solution.py:69
  62.5 8.4 %collective-permute-start.6 = (bf16[384,1152]{1,0:T(8,128)(2,1)S(1)}, bf16[384,1152]{1,0:T(8,128)(2,1)}, u32[]{:S(2)}, u32[]{:S(2)}) collective-permute-start(bf16[384,1152]{1,0:T(8,128)(2,1)S(1)} %bitcast.8), channel_id=1, source_target_pairs={{0,24},{24,0},{1,25},{25,1},{2,26},{26,2},{3,27},{27,3},{4,28},{28... | collective-permute-start | bytes 2654216 | tf_op jit(solution)/shard_map/ppermute | solution.py:69
  74.0 2.2 %copy-start.3 = (bf16[576,1280]{1,0:T(8,128)(2,1)S(1)}, bf16[576,1280]{1,0:T(8,128)(2,1)}, u32[]{:S(2)}) copy-start(bf16[576,1280]{1,0:T(8,128)(2,1)} %constant_dynamic-update-slice_fusion.3) | copy-start | bytes 4423684
  77.1 20.8 %collective-permute-start.11 = (bf16[384,1152]{1,0:T(8,128)(2,1)S(1)}, bf16[384,1152]{1,0:T(8,128)(2,1)S(1)}, u32[]{:S(2)}, u32[]{:S(2)}) collective-permute-start(bf16[384,1152]{1,0:T(8,128)(2,1)S(1)} %convolution_convert_fusion), channel_id=1, source_target_pairs={{0,24},{24,0},{1,25},{25,1},{2,26},{26,2},{3,27},{27,3},{4,28},{28... | collective-permute-start | bytes 2654216 | tf_op jit(solution)/shard_map/ppermute | solution.py:69
  79.1 18.1 %collective-permute-start.7 = (bf16[184,1152]{1,0:T(8,128)(2,1)S(1)}, bf16[184,1152]{1,0:T(8,128)(2,1)S(1)}, u32[]{:S(2)}, u32[]{:S(2)}) collective-permute-start(bf16[184,1152]{1,0:T(8,128)(2,1)S(1)} %slice.83), channel_id=1, source_target_pairs={{0,1},{1,2},{2,3},{3,4},{4,5},{5,6},{6,7},{7,0},{8,9},{9,10},{10,1... | collective-permute-start | bytes 1271816 | tf_op jit(solution)/shard_map/ppermute | solution.py:69
  83.1 13.4 %collective-permute-start.8 = (bf16[176,1152]{1,0:T(8,128)(2,1)S(1)}, bf16[176,1152]{1,0:T(8,128)(2,1)S(1)}, u32[]{:S(2)}, u32[]{:S(2)}) collective-permute-start(bf16[176,1152]{1,0:T(8,128)(2,1)S(1)} %slice.85), channel_id=1, source_target_pairs={{0,7},{1,0},{2,1},{3,2},{4,3},{5,4},{6,5},{7,6},{8,15},{9,8},{10,9... | collective-permute-start | bytes 1216520 | tf_op jit(solution)/shard_map/ppermute | solution.py:69
  99.8 16.5 %copy-start.4 = (f32[24,1]{1,0:T(8,128)S(1)}, f32[24,1]{1,0:T(8,128)}, u32[]{:S(2)}) copy-start(f32[24,1]{1,0:T(8,128)} %get-tuple-element.21) | copy-start | bytes 292
  99.8 17.1 %all-to-all-start.2 = ((bf16[4,96,1152]{2,1,0:T(8,128)(2,1)}), bf16[4,96,1152]{2,1,0:T(8,128)(2,1)S(1)}, u32[]{:S(2)}, u32[]{:S(2)}) async-start(bf16[4,96,1152]{2,1,0:T(8,128)(2,1)} %bitcast.12), calls=%async_computation.2 | async-start | bytes 1769472 | tf_op jit(solution)/shard_map/all_to_all | solution.py:48
  106.6 15.5 %collective-permute-start.9 = (bf16[72,1152]{1,0:T(8,128)(2,1)}, bf16[72,1152]{1,0:T(8,128)(2,1)}, u32[]{:S(2)}, u32[]{:S(2)}) collective-permute-start(bf16[72,1152]{1,0:T(8,128)(2,1)} %get-tuple-element.22), channel_id=1, source_target_pairs={{0,5},{1,6},{2,7},{3,0},{4,1},{5,2},{6,3},{7,4},{8,13},{9,14},{10,... | collective-permute-start | bytes 497672 | tf_op jit(solution)/shard_map/ppermute | solution.py:69
  109.5 18.3 %collective-permute-start.10 = (bf16[72,1152]{1,0:T(8,128)(2,1)}, bf16[72,1152]{1,0:T(8,128)(2,1)}, u32[]{:S(2)}, u32[]{:S(2)}) collective-permute-start(bf16[72,1152]{1,0:T(8,128)(2,1)} %get-tuple-element.23), channel_id=1, source_target_pairs={{0,3},{1,4},{2,5},{3,6},{4,7},{5,0},{6,1},{7,2},{8,11},{9,12},{10,... | collective-permute-start | bytes 497672 | tf_op jit(solution)/shard_map/ppermute | solution.py:69
  117.8 22.9 %copy-start.1 = (bf16[24,1152]{1,0:T(8,128)(2,1)S(1)}, bf16[24,1152]{1,0:T(8,128)(2,1)}, u32[]{:S(2)}) copy-start(bf16[24,1152]{1,0:T(8,128)(2,1)} %txt_ref.1) | copy-start | bytes 165892
  117.8 22.9 %copy-start.5 = (f32[24]{0:T(128)S(1)}, f32[24]{0:T(128)}, u32[]{:S(2)}) copy-start(f32[24]{0:T(128)} %reduce.3) | copy-start | bytes 292
  117.8 11.1 %all-to-all-start.3 = ((bf16[4,24,1152]{2,1,0:T(8,128)(2,1)}), bf16[4,24,1152]{2,1,0:T(8,128)(2,1)S(1)}, u32[]{:S(2)}, u32[]{:S(2)}) async-start(bf16[4,24,1152]{2,1,0:T(8,128)(2,1)} %bitcast.14), calls=%async_computation.3 | async-start | bytes 442368 | tf_op jit(solution)/shard_map/all_to_all | solution.py:48
  122.1 29.5 %copy-start = (bf16[24,1152]{1,0:T(8,128)(2,1)S(1)}, bf16[24,1152]{1,0:T(8,128)(2,1)}, u32[]{:S(2)}) copy-start(bf16[24,1152]{1,0:T(8,128)(2,1)} %img_ref.1) | copy-start | bytes 165892
  129.0 12.6 %collective-permute-start.12 = (bf16[24,1152]{1,0:T(8,128)(2,1)S(1)}, bf16[24,1152]{1,0:T(8,128)(2,1)S(1)}, u32[]{:S(2)}, u32[]{:S(2)}) collective-permute-start(bf16[24,1152]{1,0:T(8,128)(2,1)S(1)} %get-tuple-element.30), channel_id=1, source_target_pairs={{0,200},{8,208},{16,384},{192,392},{200,400},{208,576},{384,584},{... | collective-permute-start | bytes 165896 | tf_op jit(solution)/shard_map/ppermute | solution.py:69
  138.7 12.8 %collective-permute-start.13 = (bf16[24,1152]{1,0:T(8,128)(2,1)S(1)}, bf16[24,1152]{1,0:T(8,128)(2,1)S(1)}, u32[]{:S(2)}, u32[]{:S(2)}) collective-permute-start(bf16[24,1152]{1,0:T(8,128)(2,1)S(1)} %get-tuple-element.31), channel_id=1, source_target_pairs={{0,400},{8,576},{16,584},{192,592},{200,0},{208,8},{384,16},{392,1... | collective-permute-start | bytes 165896 | tf_op jit(solution)/shard_map/ppermute | solution.py:69
